TPU v7x, 512 devices: a whole 4x8x8 slice. The times are simulated.
512 devices in a mesh: grp: 8 (over y), dev: 64 (over z, x, core).
Axes of the slice: x: 4, y: 8, z: 8, core: 2. Of those that a mesh axis runs over, the one named last changes fastest.
Arguments:
- queries: bfloat16 [512, 64, 576], P(('grp', 'dev')), may hold values from -30 to 30
- lengths: int32 [512], P(('grp', 'dev')), may hold values from 1 to 768, as said below
- pages: bfloat16 [2048, 64, 576], P(('grp', 'dev')), may hold values from -7 to 7
- slot_owner: int32 [2048], P(('grp', 'dev')), may hold values from 0 to 7, as said below
- slot_page: int32 [2048], P(('grp', 'dev')), may hold values from 0 to 11, as said below
- value_up: bfloat16 [64, 512, 128], P('dev'), may hold values from -2 to 2
- out_proj: bfloat16 [8192, 7168], P('dev'), may hold values from -0.0625 to 0.0625
Outputs:
- hidden: bfloat16 [512, 7168], P(('grp', 'dev'))
Inputs may be any that keep to these rules, and one draw needn't show every extreme that they name: Request R's pages number ceil(lengths[R] / 64); in every column one request is exactly 768 tokens long. `slot_owner`: every slot holds a page; every page of every request lies in exactly one slot of the request's column, on any of its 8 devices. `slot_page`: page numbers of one request are 0 to its page count - 1, each once.
All inputs are finite; a program needn't handle non-finite values.
Results may differ from a plain program's by a relative error of at most 0.02.
Values may be sent and summed in bfloat16 or wider, within the bound.
A program may use at most 64 MiB of HBM per device.

v0:
```python
import jax
import jax.numpy as jnp
from jax import lax
from jax.sharding import PartitionSpec as P

ROPE = 64
NOPE = 128


def joined(value, axis, join):
    pieces = jax.tree.map(lambda part: lax.all_gather(part, axis), value)
    head = jax.tree.map(lambda part: part[0], pieces)
    tail = jax.tree.map(lambda part: part[1:], pieces)
    total, _ = lax.scan(lambda total, section: (join(total, section), None), head, tail)
    return total


def device_partials(column_queries, column_lengths, dev_pages, owner_ids, page_ids):
    score_scale = (NOPE + ROPE) ** (-0.5)
    column_count = column_queries.shape[0]
    slot_queries = jnp.take(column_queries, owner_ids, axis=0)
    scores = (
        jnp.einsum("shc,spc->shp", slot_queries, dev_pages, preferred_element_type=jnp.float32)
        * score_scale
    )
    page_tokens = dev_pages.shape[1]
    positions = page_ids[:, None] * page_tokens + jnp.arange(page_tokens, dtype=jnp.int32)[None, :]
    live_tokens = positions < jnp.take(column_lengths, owner_ids, axis=0)[:, None]
    masked = jnp.where(live_tokens[:, None, :], scores, jnp.float32(-1e30))
    slot_max = jnp.max(masked, axis=-1)
    pick_slot = owner_ids[None, :] == jnp.arange(column_count, dtype=jnp.int32)[:, None]
    local_max = jnp.max(
        jnp.where(pick_slot[:, :, None], slot_max[None, :, :], jnp.float32(-1e30)), axis=1
    )
    shifted = scores - jnp.take(local_max, owner_ids, axis=0)[:, :, None]
    weights = jnp.where(live_tokens[:, None, :], jnp.exp(shifted), jnp.float32(0.0))
    pick_float = pick_slot.astype(jnp.float32)
    local_total = jnp.dot(pick_float, jnp.sum(weights, axis=-1), precision=lax.Precision.HIGHEST)
    weights_bf = weights.astype(jnp.bfloat16)
    latent_width = dev_pages.shape[2] - ROPE
    slot_value = jnp.einsum(
        "shp,spl->shl",
        weights_bf,
        dev_pages[:, :, :latent_width],
        preferred_element_type=jnp.float32,
    )
    local_value = jnp.einsum("ks,shl->khl", pick_float, slot_value, precision=lax.Precision.HIGHEST)
    return (local_max, local_total, local_value)


def merge_pair(left_part, right_part):
    top_score = jnp.maximum(left_part[0], right_part[0])
    left_factor = jnp.exp(left_part[0] - top_score)
    right_factor = jnp.exp(right_part[0] - top_score)
    denominator = left_part[1] * left_factor + right_part[1] * right_factor
    weighted = left_part[2] * left_factor[..., None] + right_part[2] * right_factor[..., None]
    return (top_score, denominator, weighted)


def body(queries, lengths, pages, slot_owner, slot_page, value_up, out_proj):
    local_rows = queries.shape[0]
    column_queries, column_lengths = (
        lax.all_gather(queries, "grp", axis=0, tiled=True),
        lax.all_gather(lengths, "grp", axis=0, tiled=True),
    )
    local_max, local_total, local_value = device_partials(
        column_queries, column_lengths, pages, slot_owner, slot_page
    )
    merged = joined((local_max, local_total, local_value), "grp", merge_pair)
    first_row = lax.axis_index("grp") * local_rows
    denominator = lax.dynamic_slice_in_dim(merged[1], first_row, local_rows, 0)
    weighted = lax.dynamic_slice_in_dim(merged[2], first_row, local_rows, 0)
    latent = (weighted / denominator[..., None]).astype(jnp.bfloat16)
    head_latent = lax.all_to_all(latent, "dev", split_axis=1, concat_axis=0, tiled=True)
    head_value = jnp.einsum(
        "rhl,hlv->rhv", head_latent, value_up, preferred_element_type=jnp.float32
    ).astype(jnp.bfloat16)
    flat_value = head_value.reshape(head_value.shape[0], head_value.shape[1] * head_value.shape[2])
    summed = lax.psum_scatter(
        jnp.dot(flat_value, out_proj, preferred_element_type=jnp.float32),
        "dev",
        scatter_dimension=0,
        tiled=True,
    )
    return summed.astype(jnp.bfloat16)


def solution(mesh):
    in_specs = (
        P(("grp", "dev"), None, None),
        P(("grp", "dev")),
        P(("grp", "dev"), None, None),
        P(("grp", "dev")),
        P(("grp", "dev")),
        P("dev", None, None),
        P("dev", None),
    )
    out_specs = P(("grp", "dev"), None)
    return jax.shard_map(body, mesh=mesh, in_specs=in_specs, out_specs=out_specs, check_vma=False)
```

profile of v0, /device:TPU:1, one launch (start us, length us, event | category | flops | bytes accessed | tf_op | source)
XLA Modules:
  0.0 475.2 jit_solution(13865803867506819743)
XLA Ops:
  8.0 1.3 dynamic-slice
  9.4 0.8 dynamic-update-slice
  10.9 12.0 %all-reduce = s32[8]{0:T(128)S(1)} all-reduce(s32[8]{0:T(128)S(1)} %dynamic-update-slice), channel_id=1, replica_groups=mesh['grp'=8,'dev'=64] {'grp'}, use_global_device_ids=true, to_apply=%add | all-reduce | flops 8 | bytes 64
  24.9 20.3 %all_gather.25 = bf16[8,64,576]{2,1,0:T(8,128)(2,1)S(1)} all-gather(bf16[1,64,576]{2,1,0:T(8,128)(2,1)} %param.9), channel_id=1, replica_groups=mesh['grp'=8,'dev'=64] {'grp'}, dimensions={0}, use_global_device_ids=true | all-gather | bytes 663552 | tf_op jit(solution)/shard_map/all_gather | solution.py:63
  47.4 2.1 fusion.5
  49.5 18.4 %all-gather = f32[64,64]{1,0:T(8,128)S(1)} all-gather(f32[8,64]{1,0:T(8,128)S(1)} %select_reduce_fusion.1), channel_id=2, replica_groups=mesh['grp'=8,'dev'=64] {'grp'}, dimensions={0}, use_global_device_ids=true | all-gather | bytes 18432 | tf_op jit(solution)/shard_map/all_gather | solution.py:11
  68.3 19.7 %all-gather.1 = f32[64,64]{1,0:T(8,128)S(1)} all-gather(f32[8,64]{1,0:T(8,128)S(1)} %fusion.27), channel_id=3, replica_groups=mesh['grp'=8,'dev'=64] {'grp'}, dimensions={0}, use_global_device_ids=true | all-gather | bytes 18432 | tf_op jit(solution)/shard_map/all_gather | solution.py:11
  88.0 68.8 %all-gather.5.cloned.1.call-done = f32[64,64,512]{2,0,1:T(8,128)} async-done(((f32[8,64,512]{2,0,1:T(8,128)}), f32[64,64,512]{2,0,1:T(8,128)}) %all-gather.5.cloned.1.call-update) | async-done | bytes 8388624 | tf_op jit(solution)/shard_map/all_gather | solution.py:11
  156.8 1.2 slice-done
  158.6 7.0 %slice_bitcast_fusion = f32[7,8,64,512]{3,1,0,2:T(8,128)} fusion(f32[64,64,512]{2,0,1:T(8,128)} %all-gather.5.cloned.1.call-done), kind=kLoop, calls=%fused_computation.13 | loop fusion | bytes 14680064 | tf_op jit(solution)/shard_map/slice | solution.py:13
  165.6 15.8 %while.14 = (s32[]{:T(128)}, f32[8,64]{1,0:T(8,128)S(1)}, f32[8,64]{1,0:T(8,128)S(1)}, f32[8,64,512]{2,1,0:T(8,128)S(1)}, f32[7,8,64]{2,1,0:T(8,128)S(1)}, /*ind...) while((s32[]{:T(128)}, f32[8,64]{1,0:T(8,128)S(1)}, f32[8,64]{1,0:T(8,128)S(1)}, ...), condition=%wide.region_4.5_spmd, body=%wide.region_3.4_spmd.sunk | while | flops 789506 | bytes 5263461 | solution.py:14
  165.6 1.3 constant_dynamic-slice_fusion.2
  166.9 0.9 fusion.36
  167.9 1.3 constant_dynamic-slice_fusion.2
  169.2 0.9 fusion.36
  170.1 1.3 constant_dynamic-slice_fusion.2
  171.4 0.9 fusion.36
  172.4 1.3 constant_dynamic-slice_fusion.2
  173.7 0.9 fusion.36
  174.7 1.3 constant_dynamic-slice_fusion.2
  176.0 0.9 fusion.36
  176.9 1.3 constant_dynamic-slice_fusion.2
  178.2 0.9 fusion.36
  179.2 1.3 constant_dynamic-slice_fusion.2
  180.5 0.9 fusion.36
  182.8 1.0 reduce
  184.4 11.0 %all-to-all-start = ((bf16[64,2,256]{2,1,0:T(2,128)(2,1)}), bf16[64,2,256]{2,1,0:T(2,128)(2,1)S(1)}, u32[]{:S(2)}, u32[]{:S(2)}) async-start(bf16[64,2,256]{2,1,0:T(2,128)(2,1)} %reshape.140), calls=%async_computation | async-start | bytes 131072 | tf_op jit(solution)/shard_map/all_to_all | solution.py:74
  195.5 1.3 dynamic-slice.1
  196.7 8.8 %all-to-all-done = bf16[64,2,256]{2,1,0:T(2,128)(2,1)S(1)} async-done(((bf16[64,2,256]{2,1,0:T(2,128)(2,1)}), bf16[64,2,256]{2,1,0:T(2,128)(2,1)S(1)}, u32[]{:S(2)}, u32[]{:S(2)}) %all-to-all-start) | async-done | bytes 65568 | tf_op jit(solution)/shard_map/all_to_all | solution.py:74
  205.6 1.8 fusion.4
  207.4 259.7 %all-reduce.3 = bf16[64,7168]{1,0:T(8,128)(2,1)S(1)} all-reduce(f32[64,7168]{1,0:T(8,128)} %fusion.4), channel_id=5, replica_groups=mesh['grp'=8,'dev'=64] {'dev'}, use_global_device_ids=true, to_apply=%region_5.6.clone | all-reduce | flops 458752 | bytes 2752512
  467.2 1.2 dynamic-slice_convert_fusion
  (45 shorter events, 8.6 us)
Async XLA Ops:
  6.5 199.1 %copy-start = (bf16[128,7168]{1,0:T(8,128)(2,1)S(1)}, bf16[128,7168]{1,0:T(8,128)(2,1)}, u32[]{:S(2)}) copy-start(bf16[128,7168]{1,0:T(8,128)(2,1)} %param.15) | copy-start | bytes 5505028
  6.5 39.4 %copy-start.1 = (bf16[4,64,576]{2,1,0:T(8,128)(2,1)S(1)}, bf16[4,64,576]{2,1,0:T(8,128)(2,1)}, u32[]{:S(2)}) copy-start(bf16[4,64,576]{2,1,0:T(8,128)(2,1)} %param.11) | copy-start | bytes 884740
  6.5 150.2 %all-gather.5.cloned.1.call-start = ((), (), s32[]{:S(2)}) async-start(), calls=%async_computation.1 | async-start | bytes 9437184 | tf_op jit(solution)/shard_map/all_gather | solution.py:11
  23.5 23.8 %copy-start.3 = (s32[4]{0:T(128)S(1)}, s32[4]{0:T(128)}, u32[]{:S(2)}) copy-start(s32[4]{0:T(128)} %param.12) | copy-start | bytes 52
  156.8 1.2 slice-start
  181.4 24.2 %copy-start.2 = (bf16[1,512,128]{2,1,0:T(8,128)(2,1)S(1)}, bf16[1,512,128]{2,1,0:T(8,128)(2,1)}, u32[]{:S(2)}) copy-start(bf16[1,512,128]{2,1,0:T(8,128)(2,1)} %param.14) | copy-start | bytes 393220
  184.4 21.1 %all-to-all-start = ((bf16[64,2,256]{2,1,0:T(2,128)(2,1)}), bf16[64,2,256]{2,1,0:T(2,128)(2,1)S(1)}, u32[]{:S(2)}, u32[]{:S(2)}) async-start(bf16[64,2,256]{2,1,0:T(2,128)(2,1)} %reshape.140), calls=%async_computation | async-start | bytes 131072 | tf_op jit(solution)/shard_map/all_to_all | solution.py:74
Sparse Core Ops, SparseCore 0:
  49.6 107.1 all-gather.4
where the time goes:
time: 480 us; the launch traced here: 475 us
  blocking collectives  330 us (69%)
  waiting for transfers between devices  77.6 us (16%)
  local copies, waits for them, and re-layouts  26.2 us (5%)
  between operations  14.3 us (3%)
  starting transfers between devices  11 us (2%)
  other arithmetic  10.9 us (2%)
  matrix products  4.82 us (1%)
    unnamed x2, blocking collectives  272 us
    all_gather x1, waiting for transfers between devices, joined(): pieces = jax.tree.map(lambda part: lax.all_gather(part, axis), value)  68.8 us
    all_gather x2, blocking collectives, joined(): pieces = jax.tree.map(lambda part: lax.all_gather(part, axis), value)  38.1 us
    all_gather x1, blocking collectives, body(): lax.all_gather(queries, 'grp', axis=0, tiled=True)  20.3 us
    all_to_all x1, starting transfers between devices, body(): lax.all_to_all(latent, 'dev', split_axis=1, concat_axis=0, tiled=True)  11 us
  transfers between devices with their start and end apart: 2, of which 2 were waited for; matrix products, arithmetic and copies ran while one was open for 0% of the time, Pallas kernels for 0%

commit v1 on v0

v1 whole, which is shorter than its diff:
```python
import jax
import jax.numpy as jnp
from jax import lax
from jax.experimental import pallas as pl
from jax.experimental.pallas import tpu as pltpu
from jax.sharding import PartitionSpec as P

MESH = pl.DeviceIdType.MESH
F32 = jnp.float32
BF16 = jnp.bfloat16

ROPE = 64
NOPE = 128
SCALE = (NOPE + ROPE) ** -0.5
NEG = -1e30

GRP = 8
NZ = 8
NS = 8
NX = 4
HEADS = 64
LAT = 512
CACHE = 576
WIDE = 640
PAGE = 64
POOL = 4
TOK = POOL * PAGE
VDIM = 128
D = 7168
HALF = D // 2
TILES = D // 128
CHUNK = 1024
NCH = D // CHUNK


def pieces(value):
    high = value.astype(BF16).astype(F32)
    rest = value - high
    mid = rest.astype(BF16).astype(F32)
    return high, mid, rest - mid


def kernel(q_hbm, len_ref, pages_hbm, owner_ref, page_ref, vup_hbm, oproj_hbm, out_ref,
           q_raw, q_own, q_in, pages, vup, oproj, part_out, part_in,
           c1_out, c1_in, c1_f, c2_out, c2_in,
           own_f, e1_out, e1_in, e2_out, e2_in, e3_f, e3_out, e3_in,
           loc_sem, qs_sem, qr_sem, ps_sem, pr_sem, c1s_sem, c1r_sem, c2s_sem, c2r_sem,
           e1s_sem, e1r_sem, e2s_sem, e2r_sem, e3s_sem, e3r_sem):
    g = lax.axis_index("grp")
    d = lax.axis_index("dev")
    z = d // NS
    s = d % NS
    x = s // 2
    c = s % 2

    def grp_peer(k):
        return (lax.rem(g + k, GRP), d)

    def z_peer(k):
        return (g, lax.rem(z + k, NZ) * NS + s)

    def s_peer(k):
        return (g, z * NS + lax.rem(s + k, NS))

    barrier = pltpu.get_barrier_semaphore()
    for k in range(1, 8):
        for peer in (grp_peer(k), z_peer(k), s_peer(k)):
            pl.semaphore_signal(barrier, inc=1, device_id=peer, device_id_type=MESH)

    q_load = pltpu.make_async_copy(q_hbm.at[0], q_raw, loc_sem.at[0])
    q_load.start()
    pages_load = pltpu.make_async_copy(pages_hbm, pages, loc_sem.at[1])
    pages_load.start()
    vup_load = pltpu.make_async_copy(vup_hbm.at[0], vup, loc_sem.at[2])
    vup_load.start()
    oproj_load = pltpu.make_async_copy(oproj_hbm, oproj, loc_sem.at[3])
    oproj_load.start()

    q_load.wait()
    length = len_ref[0]
    len_high = (length // 32).astype(F32)
    len_low = (length % 32).astype(F32)
    lane64 = lax.broadcasted_iota(jnp.int32, (HEADS, 128), 1)
    tail = jnp.concatenate([q_raw[:, LAT:CACHE].astype(F32), jnp.zeros((HEADS, WIDE - CACHE), F32)], axis=1)
    tail = jnp.where(lane64 == ROPE, len_high, jnp.where(lane64 == ROPE + 1, len_low, tail))
    q_own[:, 0:LAT] = q_raw[:, 0:LAT]
    q_own[:, LAT:WIDE] = tail.astype(BF16)

    pl.semaphore_wait(barrier, 21)

    def remote(src, dst, send, recv, peer):
        copy = pltpu.make_async_remote_copy(
            src_ref=src, dst_ref=dst, send_sem=send, recv_sem=recv,
            device_id=peer, device_id_type=MESH)
        copy.start()
        return copy

    order = (1, 7, 2, 6, 3, 5, 4)
    q_copies = {k: remote(q_own, q_in.at[k], qs_sem.at[k], qr_sem.at[k], grp_peer(k)) for k in order}

    pages_load.wait()
    lane = lax.broadcasted_iota(jnp.int32, (1, TOK), 1)
    slot = lane // PAGE
    owner_v = jnp.zeros((1, TOK), jnp.int32)
    first_v = jnp.zeros((1, TOK), jnp.int32)
    for i in range(POOL):
        owner_v = jnp.where(slot == i, owner_ref[i], owner_v)
        first_v = jnp.where(slot == i, page_ref[i], first_v)
    pos_v = (first_v * PAGE + lane % PAGE).astype(F32)

    def partial(q_ref, request):
        page_all = pages[...].reshape(TOK, CACHE)
        query = q_ref[:, 0:CACHE]
        scores = lax.dot_general(query, page_all, (((1,), (1,)), ((), ())),
                                 preferred_element_type=F32) * SCALE
        side = q_ref[:, LAT:WIDE].astype(F32)
        limit = side[:, ROPE:ROPE + 1] * 32.0 + side[:, ROPE + 1:ROPE + 2]
        live = (pos_v < limit) & (owner_v == request)
        top = jnp.max(jnp.where(live, scores, NEG), axis=1, keepdims=True)
        weights = jnp.where(live, jnp.exp(scores - top), 0.0)
        total = jnp.sum(weights, axis=1, keepdims=True)
        value = jnp.dot(weights.astype(BF16), page_all[:, 0:LAT], preferred_element_type=F32)
        return top, total, value

    part_copies = {}
    for k in order:
        q_copies[k].wait_recv()
        top, total, value = partial(q_in.at[k], lax.rem(g + (GRP - k), GRP))
        part_out[k, :, 0:LAT] = value.astype(BF16)
        top_p = pieces(top)
        total_p = pieces(total)
        stats = jnp.zeros((HEADS, 128), F32)
        for at, piece in enumerate(top_p + total_p):
            stats = jnp.where(lane64 == at, piece, stats)
        part_out[k, :, LAT:WIDE] = stats.astype(BF16)
        part_copies[k] = remote(part_out.at[k], part_in.at[k], ps_sem.at[k], pr_sem.at[k], grp_peer(GRP - k))

    top0, total0, value0 = partial(q_own, g)

    tops, totals = {0: top0}, {0: total0}
    best = top0
    for k in order:
        part_copies[k].wait_recv()
        stats = part_in[k, :, LAT:WIDE].astype(F32)
        tops[k] = (stats[:, 0:1] + stats[:, 1:2]) + stats[:, 2:3]
        totals[k] = (stats[:, 3:4] + stats[:, 4:5]) + stats[:, 5:6]
        best = jnp.maximum(best, tops[k])
    factor = jnp.exp(top0 - best)
    denominator = factor * total0
    merged = factor * value0
    for k in order:
        factor = jnp.exp(tops[k] - best)
        denominator = denominator + factor * totals[k]
        merged = merged + factor * part_in[k, :, 0:LAT].astype(F32)
    latent = merged * (1.0 / denominator)

    for zz in range(NZ):
        rows = latent[zz * NS:(zz + 1) * NS, :]
        c1_out[zz] = jnp.concatenate([rows[:, 0:256], rows[:, 256:512]], axis=0).astype(BF16)
    c1_copies = []
    for k in order:
        to = lax.rem(z + k, NZ)
        c1_copies.append(remote(c1_out.at[to], c1_in.at[z], c1s_sem.at[k], c1r_sem.at[k], z_peer(k)))
    c1_in[z] = c1_out[z]
    for copy in c1_copies:
        copy.wait_recv()
    arrived = c1_in[...].astype(F32).reshape(NZ * 16, 256)
    c1_f[0] = arrived[:, 0:128]
    c1_f[1] = arrived[:, 128:256]
    for ss in range(NS):
        quarters = [[c1_f[col, pl.ds(half * 8 + ss, NZ, stride=16), :] for col in range(2)] for half in range(2)]
        c2_out[ss] = jnp.concatenate([jnp.concatenate(pair, axis=1) for pair in quarters], axis=0).astype(BF16)
    c2_copies = []
    for k in order:
        to = lax.rem(s + k, NS)
        c2_copies.append(remote(c2_out.at[to], c2_in.at[s], c2s_sem.at[k], c2r_sem.at[k], s_peer(k)))
    c2_in[s] = c2_out[s]
    vup_load.wait()
    for copy in c2_copies:
        copy.wait_recv()

    blocks = []
    for dc in (1, 0):
        for dx in range(NX):
            at = lax.rem(x + dx, NX) * 2 + lax.rem(c + dc, 2)
            both = c2_in[at].astype(F32)
            blocks.append(jnp.concatenate([both[0:8, :], both[8:16, :]], axis=1))
    heads_in = jnp.concatenate(blocks, axis=0).astype(BF16)
    head_value = jnp.dot(heads_in, vup[...], preferred_element_type=F32).astype(BF16)

    oproj_load.wait()
    core_peer = (g, z * NS + x * 2 + (1 - c))
    e1_copies = []
    for n in range(NCH):
        cols = slice(n * CHUNK, (n + 1) * CHUNK)
        product = jnp.dot(head_value, oproj[:, cols], preferred_element_type=F32)
        e1_out[n] = product[0:32].astype(BF16)
        e1_copies.append(remote(e1_out.at[n], e1_in.at[n], e1s_sem.at[n], e1r_sem.at[n], core_peer))
        own_f[n] = product[32:64]

    for n in range(NCH):
        e1_copies[n].wait_recv()
        both = own_f[n] + e1_in[n].astype(F32)
        own_f[n] = both
        for t in range(CHUNK // 512):
            tile = n * (CHUNK // 512) + t
            half, col = tile // (HALF // 512), tile % (HALF // 512) * 512
            for dx in range(1, NX):
                e2_out[dx, half * 8:(half + 1) * 8, col:col + 512] = both[dx * 8:(dx + 1) * 8, t * 512:(t + 1) * 512].astype(BF16)
    e2_copies = {}
    for dx in (1, 3, 2):
        peer = (g, z * NS + lax.rem(x + dx, NX) * 2 + c)
        e2_copies[dx] = remote(e2_out.at[dx], e2_in.at[dx], e2s_sem.at[dx], e2r_sem.at[dx], peer)
    for dx in (1, 3, 2):
        e2_copies[dx].wait_recv()
    for tile in range(TILES):
        n, t = tile // (CHUNK // 128), tile % (CHUNK // 128)
        half, col = tile // (TILES // 2), tile % (TILES // 2) * 128
        total = own_f[n, 0:8, t * 128:(t + 1) * 128]
        for dx in (1, 3, 2):
            total = total + e2_in[dx, half * 8:(half + 1) * 8, col:col + 128].astype(F32)
        e3_f[tile * 8:(tile + 1) * 8, :] = total

    for zz in range(NZ):
        e3_out[zz] = jnp.concatenate(
            [e3_f[pl.ds(zz, TILES, stride=8), :], jnp.zeros((8, 128), F32)], axis=0).astype(BF16)
    e3_copies = []
    for k in order:
        to = lax.rem(z + k, NZ)
        e3_copies.append(remote(e3_out.at[to], e3_in.at[k], e3s_sem.at[k], e3r_sem.at[k], z_peer(k)))
    total = e3_out[z].astype(F32)
    for at, k in enumerate(order):
        e3_copies[at].wait_recv()
        total = total + e3_in[k].astype(F32)
    out_ref[...] = total[0:TILES].astype(BF16)

    for copy in list(q_copies.values()) + list(part_copies.values()) + c1_copies + c2_copies + e1_copies + list(e2_copies.values()) + e3_copies:
        copy.wait_send()


def body(queries, lengths, pages, slot_owner, slot_page, value_up, out_proj):
    any_spec = pl.BlockSpec(memory_space=pl.ANY)
    smem = pl.BlockSpec(memory_space=pltpu.SMEM)
    dma = pltpu.SemaphoreType.DMA
    result = pl.pallas_call(
        kernel,
        out_shape=jax.ShapeDtypeStruct((TILES, 128), BF16),
        in_specs=[any_spec, smem, any_spec, smem, smem, any_spec, any_spec],
        out_specs=pl.BlockSpec(memory_space=pltpu.VMEM),
        scratch_shapes=[
            pltpu.VMEM((HEADS, CACHE), BF16),
            pltpu.VMEM((HEADS, WIDE), BF16),
            pltpu.VMEM((GRP, HEADS, WIDE), BF16),
            pltpu.VMEM((POOL, PAGE, CACHE), BF16),
            pltpu.VMEM((LAT, VDIM), BF16),
            pltpu.VMEM((VDIM, D), BF16),
            pltpu.VMEM((GRP, HEADS, WIDE), BF16),
            pltpu.VMEM((GRP, HEADS, WIDE), BF16),
            pltpu.VMEM((NZ, 16, 256), BF16),
            pltpu.VMEM((NZ, 16, 256), BF16),
            pltpu.VMEM((2, NZ * 16, 128), F32),
            pltpu.VMEM((NS, 16, 256), BF16),
            pltpu.VMEM((NS, 16, 256), BF16),
            pltpu.VMEM((NCH, 32, CHUNK), F32),
            pltpu.VMEM((NCH, 32, CHUNK), BF16),
            pltpu.VMEM((NCH, 32, CHUNK), BF16),
            pltpu.VMEM((NX, 16, HALF), BF16),
            pltpu.VMEM((NX, 16, HALF), BF16),
            pltpu.VMEM((TILES * 8, 128), F32),
            pltpu.VMEM((NZ, 64, 128), BF16),
            pltpu.VMEM((NZ, 64, 128), BF16),
            dma((4,)),
            dma((8,)), dma((8,)), dma((8,)), dma((8,)),
            dma((8,)), dma((8,)), dma((8,)), dma((8,)),
            dma((NCH,)), dma((NCH,)), dma((NX,)), dma((NX,)), dma((8,)), dma((8,)),
        ],
        compiler_params=pltpu.CompilerParams(
            collective_id=0, has_side_effects=True, vmem_limit_bytes=60 * 1024 * 1024),
    )(queries, lengths, pages, slot_owner, slot_page, value_up, out_proj)
    return result.reshape(1, D)


def solution(mesh):
    in_specs = (
        P(("grp", "dev"), None, None),
        P(("grp", "dev")),
        P(("grp", "dev"), None, None),
        P(("grp", "dev")),
        P(("grp", "dev")),
        P("dev", None, None),
        P("dev", None),
    )
    out_specs = P(("grp", "dev"), None)
    return jax.shard_map(body, mesh=mesh, in_specs=in_specs, out_specs=out_specs, check_vma=False)
```

time: 480 us -> 75.8 us (0.16)
  blocking collectives: 330 us -> 0 us
  waiting for transfers between devices: 77.6 us -> 0 us
  Pallas kernels: 0 us -> 73.6 us
  local copies, waits for them, and re-layouts: 26.2 us -> 1.34 us
  between operations: 14.3 us -> 0.66 us
  starting transfers between devices: 11 us -> 0 us
  other arithmetic: 10.9 us -> 0 us
  matrix products: 4.82 us -> 0 us
    unnamed x2 -> x0, blocking collectives: 272 us -> none
    pallas_call x0 -> x1, Pallas kernels: none -> 73.6 us  [body(): pl.pallas_call(kernel, out_shape=jax.ShapeDtypeStruct((TILES, 128), BF16)...]
    all_gather x1 -> x0, waiting for transfers between devices: 68.8 us -> none  [joined(): pieces = jax.tree.map(lambda part: lax.all_gather(part, axis), value)]
    all_gather x3 -> x0, blocking collectives: 58.5 us -> none  [the longest x2 38.1 us: joined(): pieces = jax.tree.map(lambda part: lax.all_gather(part, axis), value)]
    all_to_all x1 -> x0, starting transfers between devices: 11 us -> none  [body(): lax.all_to_all(latent, 'dev', split_axis=1, concat_axis=0, tiled=True)]
    dynamic_slice x7 -> x0, local copies, waits for them, and re-layouts: 9.1 us -> none  [joined(): lax.scan(lambda total, section: (join(total, section), None), head, tail)]
    all_to_all x1 -> x0, waiting for transfers between devices: 8.81 us -> none  [body(): lax.all_to_all(latent, 'dev', split_axis=1, concat_axis=0, tiled=True)]
    slice x7 -> x0, local copies, waits for them, and re-layouts: 8.21 us -> none  [the longest x3 6.98 us: joined(): tail = jax.tree.map(lambda part: part[1:], pieces)]
  transfers between devices with their start and end apart: 2 -> 0, of which waited for: 2 -> 0; matrix products, arithmetic and copies ran while one was open for 0% -> 0% of each run, Pallas kernels for 0% -> 0%
where the time goes in v1:
time: 75.8 us; the launch traced here: 75.6 us
  Pallas kernels  73.6 us (97%)
  local copies, waits for them, and re-layouts  1.34 us (2%)
    pallas_call x1, Pallas kernels, body(): pl.pallas_call(kernel, out_shape=jax.ShapeDtypeStruct((TILES, 128), BF16)...  73.6 us

profile of v1, /device:TPU:1, one launch (start us, length us, event | category | flops | bytes accessed | tf_op | source)
XLA Modules:
  0.0 75.6 jit_solution(9500110310202411057)
XLA Ops:
  0.7 73.6 %shard_map.73 = bf16[56,128]{1,0:T(8,128)(2,1)} custom-call(bf16[1,64,576]{2,1,0:T(8,128)(2,1)} %q_hbm.1, s32[1]{0:T(128)S(6)} %copy.11.len_ref, bf16[4,64,576]{2,1,0:T(8,128)(2,1)} %pages_hbm.1, s32[4]{0:T(128)} %owner_ref.1, s32[4]{0:T(128)} %page_ref.1, bf16[1,512,128]{2,1,0:T(8,128)(2,1)} %vup_hbm.1, bf16[128,7168]{1,0:T(8,128)(2,1)} %oproj_hbm.1), custom_call_target="tpu_custom_call" | custom-call | tf_op jit(solution)/shard_map/pallas_call | solution.py:245
  74.3 1.3 %copy.10 = bf16[1,1,56,128]{3,1,2,0:T(2,128)(2,1)} copy(bf16[1,1,56,128]{3,2,1,0:T(8,128)(2,1)} %bitcast.5) | data formatting | bytes 28672

commit v2 on v1

--- a/solution.py
+++ b/solution.py
@@ -21,10 +21,11 @@
 HEADS = 64
 LAT = 512
 CACHE = 576
-WIDE = 640
+HH = HEADS // 2
+PACK = 144
 PAGE = 64
 POOL = 4
-TOK = POOL * PAGE
+TOK = 2 * POOL * PAGE
 VDIM = 128
 D = 7168
 HALF = D // 2
@@ -41,10 +42,10 @@
 
 
 def kernel(q_hbm, len_ref, pages_hbm, owner_ref, page_ref, vup_hbm, oproj_hbm, out_ref,
-           q_raw, q_own, q_in, pages, vup, oproj, part_out, part_in,
+           q_raw, q_own, q_in, meta_own, meta_in, pages, vup, oproj, part_out, part_in,
            c1_out, c1_in, c1_f, c2_out, c2_in,
            own_f, e1_out, e1_in, e2_out, e2_in, e3_f, e3_out, e3_in,
-           loc_sem, qs_sem, qr_sem, ps_sem, pr_sem, c1s_sem, c1r_sem, c2s_sem, c2r_sem,
+           loc_sem, ms_sem, mr_sem, gs_sem, gr_sem, qs_sem, qr_sem, ps_sem, pr_sem, c1s_sem, c1r_sem, c2s_sem, c2r_sem,
            e1s_sem, e1r_sem, e2s_sem, e2r_sem, e3s_sem, e3r_sem):
     g = lax.axis_index("grp")
     d = lax.axis_index("dev")
@@ -69,22 +70,28 @@
 
     q_load = pltpu.make_async_copy(q_hbm.at[0], q_raw, loc_sem.at[0])
     q_load.start()
-    pages_load = pltpu.make_async_copy(pages_hbm, pages, loc_sem.at[1])
+    pages_load = pltpu.make_async_copy(pages_hbm, pages.at[0:POOL], loc_sem.at[1])
     pages_load.start()
     vup_load = pltpu.make_async_copy(vup_hbm.at[0], vup, loc_sem.at[2])
     vup_load.start()
     oproj_load = pltpu.make_async_copy(oproj_hbm, oproj, loc_sem.at[3])
     oproj_load.start()
 
+    lane = lax.broadcasted_iota(jnp.int32, (1, 128), 1)
+    meta = jnp.where(lane == 0, len_ref[0], 0)
+    for i in range(POOL):
+        meta = jnp.where(lane == 1 + i, owner_ref[i], meta)
+        meta = jnp.where(lane == 1 + POOL + i, page_ref[i], meta)
+    meta_own[...] = meta
+
     q_load.wait()
-    length = len_ref[0]
-    len_high = (length // 32).astype(F32)
-    len_low = (length % 32).astype(F32)
-    lane64 = lax.broadcasted_iota(jnp.int32, (HEADS, 128), 1)
-    tail = jnp.concatenate([q_raw[:, LAT:CACHE].astype(F32), jnp.zeros((HEADS, WIDE - CACHE), F32)], axis=1)
-    tail = jnp.where(lane64 == ROPE, len_high, jnp.where(lane64 == ROPE + 1, len_low, tail))
-    q_own[:, 0:LAT] = q_raw[:, 0:LAT]
-    q_own[:, LAT:WIDE] = tail.astype(BF16)
+    for half in range(2):
+        rows = slice(half * HH, (half + 1) * HH)
+        for j in range(4):
+            q_own[half, j * HH:(j + 1) * HH, :] = q_raw[rows, j * 128:(j + 1) * 128]
+        rope = q_raw[rows, LAT:CACHE].astype(F32)
+        q_own[half, 4 * HH:PACK, :] = jnp.concatenate([rope[0:16], rope[16:32]], axis=1).astype(BF16)
+    pages_load.wait()
 
     pl.semaphore_wait(barrier, 21)
 
@@ -95,27 +102,40 @@
         copy.start()
         return copy
 
-    order = (1, 7, 2, 6, 3, 5, 4)
-    q_copies = {k: remote(q_own, q_in.at[k], qs_sem.at[k], qr_sem.at[k], grp_peer(k)) for k in order}
-
-    pages_load.wait()
-    lane = lax.broadcasted_iota(jnp.int32, (1, TOK), 1)
-    slot = lane // PAGE
+    parity = lax.rem(g, 2)
+    order = (4, 3, 5, 2, 6, 1, 7)
+    q_copies, meta_copies, page_copies = {}, {}, []
+    for k in order:
+        meta_copies[k] = remote(meta_own, meta_in.at[k], ms_sem.at[k], mr_sem.at[k], grp_peer(k))
+    for k in order:
+        if k == 2:
+            page_copies.append(remote(pages.at[0:2], pages.at[4:6], gs_sem.at[0], gr_sem.at[0], grp_peer(1)))
+            page_copies.append(remote(pages.at[2:4], pages.at[6:8], gs_sem.at[1], gr_sem.at[1], grp_peer(7)))
+        q_copies[k] = remote(q_own.at[lax.rem(g + k, 2)], q_in.at[k], qs_sem.at[k], qr_sem.at[k], grp_peer(k))
+
+    for k in order:
+        meta_copies[k].wait_recv()
+    for copy in page_copies:
+        copy.wait_recv()
+    token = lax.broadcasted_iota(jnp.int32, (1, TOK), 1)
+    slot = token // PAGE
     owner_v = jnp.zeros((1, TOK), jnp.int32)
     first_v = jnp.zeros((1, TOK), jnp.int32)
-    for i in range(POOL):
-        owner_v = jnp.where(slot == i, owner_ref[i], owner_v)
-        first_v = jnp.where(slot == i, page_ref[i], first_v)
-    pos_v = (first_v * PAGE + lane % PAGE).astype(F32)
-
-    def partial(q_ref, request):
+    rows = [(meta, i) for i in range(POOL)] + [(meta_in[1], 0), (meta_in[1], 1), (meta_in[7], 2), (meta_in[7], 3)]
+    for i, (row, at) in enumerate(rows):
+        owner_v = jnp.where(slot == i, row[:, 1 + at:2 + at], owner_v)
+        first_v = jnp.where(slot == i, row[:, 1 + POOL + at:2 + POOL + at], first_v)
+    pos_v = first_v * PAGE + token % PAGE
+    lane16 = lax.broadcasted_iota(jnp.int32, (16, 128), 1)
+
+    def partial(packed, length, request):
         page_all = pages[...].reshape(TOK, CACHE)
-        query = q_ref[:, 0:CACHE]
+        rope = packed[4 * HH:PACK, :].astype(F32)
+        rope = jnp.concatenate([rope[:, 0:64], rope[:, 64:128]], axis=0).astype(BF16)
+        query = jnp.concatenate([packed[j * HH:(j + 1) * HH, :] for j in range(4)] + [rope], axis=1)
         scores = lax.dot_general(query, page_all, (((1,), (1,)), ((), ())),
                                  preferred_element_type=F32) * SCALE
-        side = q_ref[:, LAT:WIDE].astype(F32)
-        limit = side[:, ROPE:ROPE + 1] * 32.0 + side[:, ROPE + 1:ROPE + 2]
-        live = (pos_v < limit) & (owner_v == request)
+        live = (pos_v < length) & (owner_v == request)
         top = jnp.max(jnp.where(live, scores, NEG), axis=1, keepdims=True)
         weights = jnp.where(live, jnp.exp(scores - top), 0.0)
         total = jnp.sum(weights, axis=1, keepdims=True)
@@ -125,38 +145,42 @@
     part_copies = {}
     for k in order:
         q_copies[k].wait_recv()
-        top, total, value = partial(q_in.at[k], lax.rem(g + (GRP - k), GRP))
-        part_out[k, :, 0:LAT] = value.astype(BF16)
-        top_p = pieces(top)
-        total_p = pieces(total)
-        stats = jnp.zeros((HEADS, 128), F32)
-        for at, piece in enumerate(top_p + total_p):
-            stats = jnp.where(lane64 == at, piece, stats)
-        part_out[k, :, LAT:WIDE] = stats.astype(BF16)
+        top, total, value = partial(q_in[k], meta_in[k][:, 0:1], lax.rem(g + (GRP - k), GRP))
+        for j in range(4):
+            part_out[k, j * HH:(j + 1) * HH, :] = value[:, j * 128:(j + 1) * 128].astype(BF16)
+        stats = jnp.zeros((16, 128), F32)
+        for at, piece in enumerate(pieces(top) + pieces(total)):
+            stats = jnp.where(lane16 == at, piece[0:16], stats)
+            stats = jnp.where(lane16 == at + 6, piece[16:32], stats)
+        part_out[k, 4 * HH:PACK, :] = stats.astype(BF16)
         part_copies[k] = remote(part_out.at[k], part_in.at[k], ps_sem.at[k], pr_sem.at[k], grp_peer(GRP - k))
 
-    top0, total0, value0 = partial(q_own, g)
-
-    tops, totals = {0: top0}, {0: total0}
-    best = top0
-    for k in order:
+    own = partial(q_own[parity], meta[:, 0:1], g)
+
+    def arrived(k):
+        if k == 0:
+            return own
         part_copies[k].wait_recv()
-        stats = part_in[k, :, LAT:WIDE].astype(F32)
-        tops[k] = (stats[:, 0:1] + stats[:, 1:2]) + stats[:, 2:3]
-        totals[k] = (stats[:, 3:4] + stats[:, 4:5]) + stats[:, 5:6]
-        best = jnp.maximum(best, tops[k])
-    factor = jnp.exp(top0 - best)
-    denominator = factor * total0
-    merged = factor * value0
-    for k in order:
-        factor = jnp.exp(tops[k] - best)
-        denominator = denominator + factor * totals[k]
-        merged = merged + factor * part_in[k, :, 0:LAT].astype(F32)
-    latent = merged * (1.0 / denominator)
-
-    for zz in range(NZ):
-        rows = latent[zz * NS:(zz + 1) * NS, :]
-        c1_out[zz] = jnp.concatenate([rows[:, 0:256], rows[:, 256:512]], axis=0).astype(BF16)
+        stats = part_in[k, 4 * HH:PACK, :].astype(F32)
+        stats = jnp.concatenate([stats[:, 0:6], stats[:, 6:12]], axis=0)
+        value = jnp.concatenate([part_in[k, j * HH:(j + 1) * HH, :] for j in range(4)], axis=1).astype(F32)
+        return ((stats[:, 0:1] + stats[:, 1:2]) + stats[:, 2:3],
+                (stats[:, 3:4] + stats[:, 4:5]) + stats[:, 5:6], value)
+
+    for members, half in (((0, 4, 2, 6), parity), ((3, 5, 1, 7), 1 - parity)):
+        parts = [arrived(k) for k in members]
+        best = parts[0][0]
+        for top, _, _ in parts[1:]:
+            best = jnp.maximum(best, top)
+        denominator, merged = 0.0, 0.0
+        for top, total, value in parts:
+            factor = jnp.exp(top - best)
+            denominator = denominator + factor * total
+            merged = merged + factor * value
+        latent = merged * (1.0 / denominator)
+        for i in range(NZ // 2):
+            rows = latent[i * NS:(i + 1) * NS, :]
+            c1_out[half * (NZ // 2) + i] = jnp.concatenate([rows[:, 0:256], rows[:, 256:512]], axis=0).astype(BF16)
     c1_copies = []
     for k in order:
         to = lax.rem(z + k, NZ)
@@ -164,9 +188,9 @@
     c1_in[z] = c1_out[z]
     for copy in c1_copies:
         copy.wait_recv()
-    arrived = c1_in[...].astype(F32).reshape(NZ * 16, 256)
-    c1_f[0] = arrived[:, 0:128]
-    c1_f[1] = arrived[:, 128:256]
+    latents = c1_in[...].astype(F32).reshape(NZ * 16, 256)
+    c1_f[0] = latents[:, 0:128]
+    c1_f[1] = latents[:, 128:256]
     for ss in range(NS):
         quarters = [[c1_f[col, pl.ds(half * 8 + ss, NZ, stride=16), :] for col in range(2)] for half in range(2)]
         c2_out[ss] = jnp.concatenate([jnp.concatenate(pair, axis=1) for pair in quarters], axis=0).astype(BF16)
@@ -234,7 +258,7 @@
         total = total + e3_in[k].astype(F32)
     out_ref[...] = total[0:TILES].astype(BF16)
 
-    for copy in list(q_copies.values()) + list(part_copies.values()) + c1_copies + c2_copies + e1_copies + list(e2_copies.values()) + e3_copies:
+    for copy in list(q_copies.values()) + list(meta_copies.values()) + page_copies + list(part_copies.values()) + c1_copies + c2_copies + e1_copies + list(e2_copies.values()) + e3_copies:
         copy.wait_send()
 
 
@@ -249,13 +273,15 @@
         out_specs=pl.BlockSpec(memory_space=pltpu.VMEM),
         scratch_shapes=[
             pltpu.VMEM((HEADS, CACHE), BF16),
-            pltpu.VMEM((HEADS, WIDE), BF16),
-            pltpu.VMEM((GRP, HEADS, WIDE), BF16),
-            pltpu.VMEM((POOL, PAGE, CACHE), BF16),
+            pltpu.VMEM((2, PACK, 128), BF16),
+            pltpu.VMEM((GRP, PACK, 128), BF16),
+            pltpu.VMEM((1, 128), jnp.int32),
+            pltpu.VMEM((GRP, 1, 128), jnp.int32),
+            pltpu.VMEM((2 * POOL, PAGE, CACHE), BF16),
             pltpu.VMEM((LAT, VDIM), BF16),
             pltpu.VMEM((VDIM, D), BF16),
-            pltpu.VMEM((GRP, HEADS, WIDE), BF16),
-            pltpu.VMEM((GRP, HEADS, WIDE), BF16),
+            pltpu.VMEM((GRP, PACK, 128), BF16),
+            pltpu.VMEM((GRP, PACK, 128), BF16),
             pltpu.VMEM((NZ, 16, 256), BF16),
             pltpu.VMEM((NZ, 16, 256), BF16),
             pltpu.VMEM((2, NZ * 16, 128), F32),
@@ -270,6 +296,7 @@
             pltpu.VMEM((NZ, 64, 128), BF16),
             pltpu.VMEM((NZ, 64, 128), BF16),
             dma((4,)),
+            dma((8,)), dma((8,)), dma((2,)), dma((2,)),
             dma((8,)), dma((8,)), dma((8,)), dma((8,)),
             dma((8,)), dma((8,)), dma((8,)), dma((8,)),
             dma((NCH,)), dma((NCH,)), dma((NX,)), dma((NX,)), dma((8,)), dma((8,)),

time: 75.8 us -> 63.1 us (0.83)
  Pallas kernels: 73.6 us -> 60.9 us
    pallas_call x1, Pallas kernels: 73.6 us -> 60.9 us  [body(): pl.pallas_call(kernel, out_shape=jax.ShapeDtypeStruct((TILES, 128), BF16)...]
where the time goes in v2:
time: 63.1 us; the launch traced here: 62.9 us
  Pallas kernels  60.9 us (97%)
  local copies, waits for them, and re-layouts  1.34 us (2%)
  between operations  0.66 us (1%)
    pallas_call x1, Pallas kernels, body(): pl.pallas_call(kernel, out_shape=jax.ShapeDtypeStruct((TILES, 128), BF16)...  60.9 us
    unnamed x1, local copies, waits for them, and re-layouts  1.34 us

profile of v2, /device:TPU:1, one launch (start us, length us, event | category | flops | bytes accessed | tf_op | source)
XLA Modules:
  0.0 62.9 jit_solution(16827652833828611776)
XLA Ops:
  0.7 60.9 %shard_map.73 = bf16[56,128]{1,0:T(8,128)(2,1)} custom-call(bf16[1,64,576]{2,1,0:T(8,128)(2,1)} %q_hbm.1, s32[1]{0:T(128)S(6)} %copy.11.len_ref, bf16[4,64,576]{2,1,0:T(8,128)(2,1)} %pages_hbm.1, s32[4]{0:T(128)} %owner_ref.1, s32[4]{0:T(128)} %page_ref.1, bf16[1,512,128]{2,1,0:T(8,128)(2,1)} %vup_hbm.1, bf16[128,7168]{1,0:T(8,128)(2,1)} %oproj_hbm.1), custom_call_target="tpu_custom_call" | custom-call | tf_op jit(solution)/shard_map/pallas_call | solution.py:269
  61.6 1.3 %copy.10 = bf16[1,1,56,128]{3,1,2,0:T(2,128)(2,1)} copy(bf16[1,1,56,128]{3,2,1,0:T(8,128)(2,1)} %bitcast.5) | data formatting | bytes 28672

commit v3 on v2

--- a/solution.py
+++ b/solution.py
@@ -45,7 +45,7 @@
            q_raw, q_own, q_in, meta_own, meta_in, pages, vup, oproj, part_out, part_in,
            c1_out, c1_in, c1_f, c2_out, c2_in,
            own_f, e1_out, e1_in, e2_out, e2_in, e3_f, e3_out, e3_in,
-           loc_sem, ms_sem, mr_sem, gs_sem, gr_sem, qs_sem, qr_sem, ps_sem, pr_sem, c1s_sem, c1r_sem, c2s_sem, c2r_sem,
+           loc_sem, in_sem, ms_sem, mr_sem, gs_sem, gr_sem, qs_sem, qr_sem, ps_sem, pr_sem, c1s_sem, c1r_sem, c2s_sem, c2r_sem,
            e1s_sem, e1r_sem, e2s_sem, e2r_sem, e3s_sem, e3r_sem):
     g = lax.axis_index("grp")
     d = lax.axis_index("dev")
@@ -64,9 +64,9 @@
         return (g, z * NS + lax.rem(s + k, NS))
 
     barrier = pltpu.get_barrier_semaphore()
-    for k in range(1, 8):
-        for peer in (grp_peer(k), z_peer(k), s_peer(k)):
-            pl.semaphore_signal(barrier, inc=1, device_id=peer, device_id_type=MESH)
+    near = [grp_peer(1), grp_peer(7), z_peer(1), z_peer(7)] + [s_peer(k) for k in range(1, 8)]
+    for peer in near:
+        pl.semaphore_signal(barrier, inc=1, device_id=peer, device_id_type=MESH)
 
     q_load = pltpu.make_async_copy(q_hbm.at[0], q_raw, loc_sem.at[0])
     q_load.start()
@@ -84,6 +84,8 @@
         meta = jnp.where(lane == 1 + POOL + i, page_ref[i], meta)
     meta_own[...] = meta
 
+    order = (4, 3, 5, 2, 6, 1, 7)
+
     q_load.wait()
     for half in range(2):
         rows = slice(half * HH, (half + 1) * HH)
@@ -93,7 +95,9 @@
         q_own[half, 4 * HH:PACK, :] = jnp.concatenate([rope[0:16], rope[16:32]], axis=1).astype(BF16)
     pages_load.wait()
 
-    pl.semaphore_wait(barrier, 21)
+    def tell(sem, peers):
+        for peer in peers:
+            pl.semaphore_signal(sem, inc=1, device_id=peer, device_id_type=MESH)
 
     def remote(src, dst, send, recv, peer):
         copy = pltpu.make_async_remote_copy(
@@ -103,17 +107,30 @@
         return copy
 
     parity = lax.rem(g, 2)
-    order = (4, 3, 5, 2, 6, 1, 7)
     q_copies, meta_copies, page_copies = {}, {}, []
-    for k in order:
+
+    def send_query(k):
         meta_copies[k] = remote(meta_own, meta_in.at[k], ms_sem.at[k], mr_sem.at[k], grp_peer(k))
-    for k in order:
-        if k == 2:
-            page_copies.append(remote(pages.at[0:2], pages.at[4:6], gs_sem.at[0], gr_sem.at[0], grp_peer(1)))
-            page_copies.append(remote(pages.at[2:4], pages.at[6:8], gs_sem.at[1], gr_sem.at[1], grp_peer(7)))
         q_copies[k] = remote(q_own.at[lax.rem(g + k, 2)], q_in.at[k], qs_sem.at[k], qr_sem.at[k], grp_peer(k))
 
-    for k in order:
+    pl.semaphore_wait(barrier, 11)
+    tell(in_sem.at[0], [grp_peer(1), grp_peer(7)])
+    tell(in_sem.at[2], [z_peer(1), z_peer(7)])
+    send_query(1)
+    send_query(7)
+    page_copies.append(remote(pages.at[0:2], pages.at[4:6], gs_sem.at[0], gr_sem.at[0], grp_peer(1)))
+    page_copies.append(remote(pages.at[2:4], pages.at[6:8], gs_sem.at[1], gr_sem.at[1], grp_peer(7)))
+    pl.semaphore_wait(in_sem.at[0], 2)
+    tell(in_sem.at[1], [grp_peer(2), grp_peer(6)])
+    send_query(2)
+    send_query(6)
+    pl.semaphore_wait(in_sem.at[1], 2)
+    for k in (4, 3, 5):
+        send_query(k)
+    pl.semaphore_wait(in_sem.at[2], 2)
+    tell(in_sem.at[3], [z_peer(2), z_peer(6)])
+
+    for k in (1, 7):
         meta_copies[k].wait_recv()
     for copy in page_copies:
         copy.wait_recv()
@@ -128,24 +145,32 @@
     pos_v = first_v * PAGE + token % PAGE
     lane16 = lax.broadcasted_iota(jnp.int32, (16, 128), 1)
 
-    def partial(packed, length, request):
+    def partials(members):
         page_all = pages[...].reshape(TOK, CACHE)
-        rope = packed[4 * HH:PACK, :].astype(F32)
-        rope = jnp.concatenate([rope[:, 0:64], rope[:, 64:128]], axis=0).astype(BF16)
-        query = jnp.concatenate([packed[j * HH:(j + 1) * HH, :] for j in range(4)] + [rope], axis=1)
+        queries, limits, requests = [], [], []
+        for k in members:
+            packed = q_own[parity] if k == 0 else q_in[k]
+            row = meta if k == 0 else meta_in[k]
+            rope = packed[4 * HH:PACK, :].astype(F32)
+            rope = jnp.concatenate([rope[:, 0:64], rope[:, 64:128]], axis=0).astype(BF16)
+            queries.append(jnp.concatenate([packed[j * HH:(j + 1) * HH, :] for j in range(4)] + [rope], axis=1))
+            limits.append(jnp.broadcast_to(row[:, 0:1], (HH, 1)))
+            requests.append(jnp.full((HH, 1), lax.rem(g + (GRP - k), GRP), jnp.int32))
+        query = jnp.concatenate(queries, axis=0)
         scores = lax.dot_general(query, page_all, (((1,), (1,)), ((), ())),
                                  preferred_element_type=F32) * SCALE
-        live = (pos_v < length) & (owner_v == request)
+        live = (pos_v < jnp.concatenate(limits, axis=0)) & (owner_v == jnp.concatenate(requests, axis=0))
         top = jnp.max(jnp.where(live, scores, NEG), axis=1, keepdims=True)
         weights = jnp.where(live, jnp.exp(scores - top), 0.0)
         total = jnp.sum(weights, axis=1, keepdims=True)
         value = jnp.dot(weights.astype(BF16), page_all[:, 0:LAT], preferred_element_type=F32)
-        return top, total, value
+        return {k: (top[i * HH:(i + 1) * HH], total[i * HH:(i + 1) * HH], value[i * HH:(i + 1) * HH])
+                for i, k in enumerate(members)}
 
     part_copies = {}
-    for k in order:
-        q_copies[k].wait_recv()
-        top, total, value = partial(q_in[k], meta_in[k][:, 0:1], lax.rem(g + (GRP - k), GRP))
+
+    def send_partial(k, part):
+        top, total, value = part
         for j in range(4):
             part_out[k, j * HH:(j + 1) * HH, :] = value[:, j * 128:(j + 1) * 128].astype(BF16)
         stats = jnp.zeros((16, 128), F32)
@@ -155,11 +180,21 @@
         part_out[k, 4 * HH:PACK, :] = stats.astype(BF16)
         part_copies[k] = remote(part_out.at[k], part_in.at[k], ps_sem.at[k], pr_sem.at[k], grp_peer(GRP - k))
 
-    own = partial(q_own[parity], meta[:, 0:1], g)
+    for copy in (q_copies[1], q_copies[7]):
+        copy.wait_recv()
+    done = partials((1, 7, 0))
+    own = done[0]
+    for k in (1, 7):
+        send_partial(k, done[k])
+    for members in ((2, 6), (4, 3, 5)):
+        for k in members:
+            meta_copies[k].wait_recv()
+            q_copies[k].wait_recv()
+        done = partials(members)
+        for k in members:
+            send_partial(k, done[k])
 
     def arrived(k):
-        if k == 0:
-            return own
         part_copies[k].wait_recv()
         stats = part_in[k, 4 * HH:PACK, :].astype(F32)
         stats = jnp.concatenate([stats[:, 0:6], stats[:, 6:12]], axis=0)
@@ -167,27 +202,39 @@
         return ((stats[:, 0:1] + stats[:, 1:2]) + stats[:, 2:3],
                 (stats[:, 3:4] + stats[:, 4:5]) + stats[:, 5:6], value)
 
-    for members, half in (((0, 4, 2, 6), parity), ((3, 5, 1, 7), 1 - parity)):
-        parts = [arrived(k) for k in members]
-        best = parts[0][0]
-        for top, _, _ in parts[1:]:
-            best = jnp.maximum(best, top)
-        denominator, merged = 0.0, 0.0
-        for top, total, value in parts:
-            factor = jnp.exp(top - best)
-            denominator = denominator + factor * total
-            merged = merged + factor * value
-        latent = merged * (1.0 / denominator)
+    def merge(left, right):
+        top = jnp.maximum(left[0], right[0])
+        left_factor = jnp.exp(left[0] - top)
+        right_factor = jnp.exp(right[0] - top)
+        return (top, left_factor * left[1] + right_factor * right[1], left_factor * left[2] + right_factor * right[2])
+
+    def c1_copy(zz, origin):
+        return pltpu.make_async_remote_copy(
+            src_ref=c1_out.at[zz], dst_ref=c1_in.at[origin], send_sem=c1s_sem.at[zz], recv_sem=c1r_sem.at[origin],
+            device_id=(g, zz * NS + s), device_id_type=MESH)
+
+    def send_latents(state, half):
+        latent = state[2] * (1.0 / state[1])
         for i in range(NZ // 2):
             rows = latent[i * NS:(i + 1) * NS, :]
-            c1_out[half * (NZ // 2) + i] = jnp.concatenate([rows[:, 0:256], rows[:, 256:512]], axis=0).astype(BF16)
-    c1_copies = []
+            zz = half * (NZ // 2) + i
+            c1_out[zz] = jnp.concatenate([rows[:, 0:256], rows[:, 256:512]], axis=0).astype(BF16)
+
+            @pl.when(zz != z)
+            def _():
+                c1_copy(zz, z).start()
+
+    odd = merge(arrived(1), arrived(7))
+    even = merge(own, arrived(2))
+    even = merge(even, arrived(6))
+    pl.semaphore_wait(in_sem.at[3], 2)
+    odd = merge(merge(odd, arrived(3)), arrived(5))
+    send_latents(odd, 1 - parity)
+    even = merge(even, arrived(4))
+    send_latents(even, parity)
+    c1_in[z] = c1_out[z]
     for k in order:
-        to = lax.rem(z + k, NZ)
-        c1_copies.append(remote(c1_out.at[to], c1_in.at[z], c1s_sem.at[k], c1r_sem.at[k], z_peer(k)))
-    c1_in[z] = c1_out[z]
-    for copy in c1_copies:
-        copy.wait_recv()
+        c1_copy(lax.rem(z + k, NZ), lax.rem(z + k, NZ)).wait_recv()
     latents = c1_in[...].astype(F32).reshape(NZ * 16, 256)
     c1_f[0] = latents[:, 0:128]
     c1_f[1] = latents[:, 128:256]
@@ -258,8 +305,10 @@
         total = total + e3_in[k].astype(F32)
     out_ref[...] = total[0:TILES].astype(BF16)
 
-    for copy in list(q_copies.values()) + list(meta_copies.values()) + page_copies + list(part_copies.values()) + c1_copies + c2_copies + e1_copies + list(e2_copies.values()) + e3_copies:
+    for copy in list(q_copies.values()) + list(meta_copies.values()) + page_copies + list(part_copies.values()) + c2_copies + e1_copies + list(e2_copies.values()) + e3_copies:
         copy.wait_send()
+    for k in order:
+        c1_copy(lax.rem(z + k, NZ), z).wait_send()
 
 
 def body(queries, lengths, pages, slot_owner, slot_page, value_up, out_proj):
@@ -295,7 +344,7 @@
             pltpu.VMEM((TILES * 8, 128), F32),
             pltpu.VMEM((NZ, 64, 128), BF16),
             pltpu.VMEM((NZ, 64, 128), BF16),
-            dma((4,)),
+            dma((4,)), pltpu.SemaphoreType.REGULAR((4,)),
             dma((8,)), dma((8,)), dma((2,)), dma((2,)),
             dma((8,)), dma((8,)), dma((8,)), dma((8,)),
             dma((8,)), dma((8,)), dma((8,)), dma((8,)),

time: 63.1 us -> 63 us (level)
  no operation moved by 1% of the time
where the time goes in v3:
time: 63 us; the launch traced here: 62.8 us
  Pallas kernels  60.8 us (97%)
  local copies, waits for them, and re-layouts  1.34 us (2%)
  between operations  0.66 us (1%)
    pallas_call x1, Pallas kernels, body(): pl.pallas_call(kernel, out_shape=jax.ShapeDtypeStruct((TILES, 128), BF16)...  60.8 us
    unnamed x1, local copies, waits for them, and re-layouts  1.34 us

profile of v3, /device:TPU:1, one launch (start us, length us, event | category | flops | bytes accessed | tf_op | source)
XLA Modules:
  0.0 62.8 jit_solution(4654245744495023298)
XLA Ops:
  0.7 60.8 %shard_map.73 = bf16[56,128]{1,0:T(8,128)(2,1)} custom-call(bf16[1,64,576]{2,1,0:T(8,128)(2,1)} %q_hbm.1, s32[1]{0:T(128)S(6)} %copy.11.len_ref, bf16[4,64,576]{2,1,0:T(8,128)(2,1)} %pages_hbm.1, s32[4]{0:T(128)} %owner_ref.1, s32[4]{0:T(128)} %page_ref.1, bf16[1,512,128]{2,1,0:T(8,128)(2,1)} %vup_hbm.1, bf16[128,7168]{1,0:T(8,128)(2,1)} %oproj_hbm.1), custom_call_target="tpu_custom_call" | custom-call | tf_op jit(solution)/shard_map/pallas_call | solution.py:318
  61.5 1.3 %copy.10 = bf16[1,1,56,128]{3,1,2,0:T(2,128)(2,1)} copy(bf16[1,1,56,128]{3,2,1,0:T(8,128)(2,1)} %bitcast.5) | data formatting | bytes 28672

commit v4 on v3

v4 whole, which is shorter than its diff:
```python
import jax
import jax.numpy as jnp
from jax import lax
from jax.experimental import pallas as pl
from jax.experimental.pallas import tpu as pltpu
from jax.sharding import PartitionSpec as P

MESH = pl.DeviceIdType.MESH
F32 = jnp.float32
BF16 = jnp.bfloat16

ROPE = 64
NOPE = 128
SCALE = (NOPE + ROPE) ** -0.5
NEG = -1e30

GRP = 8
NZ = 8
NS = 8
NX = 4
HEADS = 64
LAT = 512
CACHE = 576
HH = HEADS // 2
PAGE = 64
POOL = 4
TOK = 2 * POOL * PAGE
VDIM = 128
D = 7168
HALF = D // 2
TILES = D // 128
NCH = 4
CHUNK = D // NCH
CT = CHUNK // 128


def pieces(value):
    high = value.astype(BF16).astype(F32)
    rest = value - high
    mid = rest.astype(BF16).astype(F32)
    return high, mid, rest - mid


def kernel(q_hbm, len_ref, pages_hbm, owner_ref, page_ref, vup_hbm, oproj_hbm, out_ref,
           q_own, q_in, meta_own, meta_in, pages, vup, oproj, part_out, part_in,
           lat, c2_out, c2_in, own_f, e1_out, e1_in, e2_out, e2_in, e3_f, e3_out, e3_in,
           loc_sem, in_sem, ms_sem, mr_sem, gs_sem, gr_sem, qs_sem, qr_sem, ps_sem, pr_sem, c2s_sem, c2r_sem,
           e1s_sem, e1r_sem, e2s_sem, e2r_sem, e3s_sem, e3r_sem):
    g = lax.axis_index("grp")
    d = lax.axis_index("dev")
    z = d // NS
    s = d % NS
    x = s // 2
    c = s % 2

    def grp_peer(k):
        return (lax.rem(g + k, GRP), d)

    def z_peer(k):
        return (g, lax.rem(z + k, NZ) * NS + s)

    def s_peer(k):
        return (g, z * NS + lax.rem(s + k, NS))

    barrier = pltpu.get_barrier_semaphore()
    near = [grp_peer(1), grp_peer(7), z_peer(1), z_peer(7)] + [s_peer(k) for k in range(1, 8)]
    for peer in near:
        pl.semaphore_signal(barrier, inc=1, device_id=peer, device_id_type=MESH)

    q_loads = [pltpu.make_async_copy(q_hbm.at[0, h * HH:(h + 1) * HH], q_own.at[h], loc_sem.at[4 + h]) for h in range(2)]
    for load in q_loads:
        load.start()
    pages_load = pltpu.make_async_copy(pages_hbm, pages.at[0:POOL], loc_sem.at[1])
    pages_load.start()
    vup_load = pltpu.make_async_copy(vup_hbm.at[0], vup, loc_sem.at[2])
    vup_load.start()
    oproj_load = pltpu.make_async_copy(oproj_hbm, oproj, loc_sem.at[3])
    oproj_load.start()

    lane = lax.broadcasted_iota(jnp.int32, (1, 128), 1)
    meta = jnp.where(lane == 0, len_ref[0], 0)
    for i in range(POOL):
        meta = jnp.where(lane == 1 + i, owner_ref[i], meta)
        meta = jnp.where(lane == 1 + POOL + i, page_ref[i], meta)
    meta_own[...] = meta

    order = (4, 3, 5, 2, 6, 1, 7)

    def tell(sem, peers):
        for peer in peers:
            pl.semaphore_signal(sem, inc=1, device_id=peer, device_id_type=MESH)

    def remote(src, dst, send, recv, peer):
        copy = pltpu.make_async_remote_copy(
            src_ref=src, dst_ref=dst, send_sem=send, recv_sem=recv,
            device_id=peer, device_id_type=MESH)
        copy.start()
        return copy

    parity = lax.rem(g, 2)
    q_copies, meta_copies, page_copies = {}, {}, []

    def send_query(k):
        meta_copies[k] = remote(meta_own, meta_in.at[k], ms_sem.at[k], mr_sem.at[k], grp_peer(k))
        q_copies[k] = remote(q_hbm.at[0, pl.ds(lax.rem(g + k, 2) * HH, HH)], q_in.at[k], qs_sem.at[k], qr_sem.at[k], grp_peer(k))

    pl.semaphore_wait(barrier, 11)
    tell(in_sem.at[0], [grp_peer(1), grp_peer(7)])
    tell(in_sem.at[2], [z_peer(1), z_peer(7)])
    send_query(1)
    send_query(7)
    page_copies.append(remote(pages_hbm.at[0:2], pages.at[4:6], gs_sem.at[0], gr_sem.at[0], grp_peer(1)))
    page_copies.append(remote(pages_hbm.at[2:4], pages.at[6:8], gs_sem.at[1], gr_sem.at[1], grp_peer(7)))
    pl.semaphore_wait(in_sem.at[0], 2)
    tell(in_sem.at[1], [grp_peer(2), grp_peer(6)])
    send_query(2)
    send_query(6)
    pl.semaphore_wait(in_sem.at[2], 2)
    tell(in_sem.at[3], [z_peer(2), z_peer(6)])
    pl.semaphore_wait(in_sem.at[1], 2)
    for k in (4, 3, 5):
        send_query(k)
    pl.semaphore_wait(in_sem.at[3], 2)
    tell(in_sem.at[4], [grp_peer(k) for k in order])

    pages_load.wait()
    for load in q_loads:
        load.wait()
    for k in (1, 7):
        meta_copies[k].wait_recv()
    for copy in page_copies:
        copy.wait_recv()
    token = lax.broadcasted_iota(jnp.int32, (1, TOK), 1)
    slot = token // PAGE
    owner_v = jnp.zeros((1, TOK), jnp.int32)
    first_v = jnp.zeros((1, TOK), jnp.int32)
    rows = [(meta, i) for i in range(POOL)] + [(meta_in[1], 0), (meta_in[1], 1), (meta_in[7], 2), (meta_in[7], 3)]
    for i, (row, at) in enumerate(rows):
        owner_v = jnp.where(slot == i, row[:, 1 + at:2 + at], owner_v)
        first_v = jnp.where(slot == i, row[:, 1 + POOL + at:2 + POOL + at], first_v)
    pos_v = first_v * PAGE + token % PAGE
    lane64 = lax.broadcasted_iota(jnp.int32, (HEADS, 128), 1)
    lane32 = lax.broadcasted_iota(jnp.int32, (HH, 128), 1)

    def partials(members):
        page_all = pages[...].reshape(TOK, CACHE)
        queries, limits, requests = [], [], []
        for k in members:
            row = meta if k == 0 else meta_in[k]
            queries.append(q_own[parity] if k == 0 else q_in[k])
            limits.append(jnp.broadcast_to(row[:, 0:1], (HH, 1)))
            requests.append(jnp.full((HH, 1), lax.rem(g + (GRP - k), GRP), jnp.int32))
        query = jnp.concatenate(queries, axis=0)
        scores = lax.dot_general(query, page_all, (((1,), (1,)), ((), ())),
                                 preferred_element_type=F32) * SCALE
        live = (pos_v < jnp.concatenate(limits, axis=0)) & (owner_v == jnp.concatenate(requests, axis=0))
        top = jnp.max(jnp.where(live, scores, NEG), axis=1, keepdims=True)
        weights = jnp.where(live, jnp.exp(scores - top), 0.0)
        total = jnp.sum(weights, axis=1, keepdims=True)
        value = jnp.dot(weights.astype(BF16), page_all[:, 0:LAT], preferred_element_type=F32)
        return {k: (top[i * HH:(i + 1) * HH], total[i * HH:(i + 1) * HH], value[i * HH:(i + 1) * HH])
                for i, k in enumerate(members)}

    def part_copy(k, i, origin):
        return pltpu.make_async_remote_copy(
            src_ref=part_out.at[k, i], dst_ref=part_in.at[k, origin],
            send_sem=ps_sem.at[k, i], recv_sem=pr_sem.at[k, origin],
            device_id=(lax.rem(g + (GRP - k), GRP), (parity * 4 + i) * NS + s), device_id_type=MESH)

    def send_partial(k, part):
        top, total, value = part
        stats = jnp.zeros((HH, 128), F32)
        for at, piece in enumerate(pieces(top) + pieces(total)):
            stats = jnp.where(lane32 == at, piece, stats)
        for i in range(4):
            rows = slice(i * 8, (i + 1) * 8)
            part_out[k, i, :, 0:256] = jnp.concatenate([value[rows, 0:256], value[rows, 256:512]], axis=0).astype(BF16)
            part_out[k, i, :, 256:384] = jnp.concatenate([stats[rows], jnp.zeros((8, 128), F32)], axis=0).astype(BF16)
        for i in range(4):
            if k == 0:
                @pl.when(parity * 4 + i != z)
                def _():
                    part_copy(k, i, z).start()

                @pl.when(parity * 4 + i == z)
                def _():
                    part_in[k, z] = part_out[k, i]
            else:
                part_copy(k, i, z).start()

    for copy in (q_copies[1], q_copies[7]):
        copy.wait_recv()
    done = partials((1, 7, 0))
    pl.semaphore_wait(in_sem.at[4], 7)
    for k in (1, 7, 0):
        send_partial(k, done[k])
    for members in ((2, 6), (4, 3, 5)):
        for k in members:
            meta_copies[k].wait_recv()
            q_copies[k].wait_recv()
        done = partials(members)
        for k in members:
            send_partial(k, done[k])

    odd = lax.rem(g + z // 4, 2)
    sources = [even_k + odd * (odd_k - even_k) for even_k, odd_k in ((0, 1), (2, 7), (6, 3), (4, 5))]
    tops, totals = [], []
    for k in sources:
        for i in range(NZ):
            @pl.when((k != 0) | (i != z))
            def _():
                part_copy(k, 0, i).wait_recv()
        stats = part_in[k, :, :, 256:384].astype(F32)[:, 0:8].reshape(HEADS, 128)
        tops.append(jnp.sum(jnp.where(lane64 < 3, stats, 0.0), axis=1, keepdims=True))
        totals.append(jnp.sum(jnp.where((lane64 >= 3) & (lane64 < 6), stats, 0.0), axis=1, keepdims=True))
    best = tops[0]
    for top in tops[1:]:
        best = jnp.maximum(best, top)
    factors = [jnp.exp(top - best) for top in tops]
    denominator = 0.0
    for factor, total in zip(factors, totals):
        denominator = denominator + factor * total
    scale = 1.0 / denominator
    factors = [factor * scale for factor in factors]
    for j in range(4):
        block = 0.0
        for k, factor in zip(sources, factors):
            both = part_in[k, :, :, j % 2 * 128:j % 2 * 128 + 128].astype(F32)
            block = block + factor * both[:, j // 2 * 8:j // 2 * 8 + 8].reshape(HEADS, 128)
        lat[j] = block

    for ss in range(NS):
        quarters = [lat[j, pl.ds(ss, NZ, stride=NS), :] for j in range(4)]
        c2_out[ss] = jnp.concatenate([jnp.concatenate(quarters[0:2], axis=1), jnp.concatenate(quarters[2:4], axis=1)], axis=0).astype(BF16)
    c2_copies = []
    for k in order:
        to = lax.rem(s + k, NS)
        c2_copies.append(remote(c2_out.at[to], c2_in.at[s], c2s_sem.at[k], c2r_sem.at[k], s_peer(k)))
    c2_in[s] = c2_out[s]
    vup_load.wait()
    for copy in c2_copies:
        copy.wait_recv()

    blocks = []
    for dc in (1, 0):
        for dx in range(NX):
            at = lax.rem(x + dx, NX) * 2 + lax.rem(c + dc, 2)
            both = c2_in[at].astype(F32)
            blocks.append(jnp.concatenate([both[0:8, :], both[8:16, :]], axis=1))
    heads_in = jnp.concatenate(blocks, axis=0).astype(BF16)
    head_value = jnp.dot(heads_in, vup[...], preferred_element_type=F32).astype(BF16)

    oproj_load.wait()
    core_peer = (g, z * NS + x * 2 + (1 - c))
    e1_copies = []
    for n in range(NCH):
        cols = slice(n * CHUNK, (n + 1) * CHUNK)
        product = jnp.dot(head_value, oproj[:, cols], preferred_element_type=F32)
        e1_out[n] = product[0:32].astype(BF16)
        e1_copies.append(remote(e1_out.at[n], e1_in.at[n], e1s_sem.at[n], e1r_sem.at[n], core_peer))
        own_f[n] = product[32:64]

    e2_copies = []
    for n in range(NCH):
        e1_copies[n].wait_recv()
        both = own_f[n] + e1_in[n].astype(F32)
        own_f[n] = both
        for dx in (2, 1, 3):
            rows = both[dx * 8:(dx + 1) * 8]
            e2_out[n, dx] = jnp.concatenate([rows[:, 0:CHUNK // 2], rows[:, CHUNK // 2:CHUNK]], axis=0).astype(BF16)
            peer = (g, z * NS + lax.rem(x + dx, NX) * 2 + c)
            e2_copies.append(remote(e2_out.at[n, dx], e2_in.at[n, dx], e2s_sem.at[n, dx], e2r_sem.at[n, dx], peer))

    e3_copies = []
    for n in range(NCH):
        for copy in e2_copies[n * 3:n * 3 + 3]:
            copy.wait_recv()
        for t in range(CT):
            half, col = t // (CT // 2), t % (CT // 2) * 128
            total = own_f[n, 0:8, t * 128:(t + 1) * 128]
            for dx in (1, 3, 2):
                total = total + e2_in[n, dx, :, col:col + 128].astype(F32)[half * 8:half * 8 + 8]
            e3_f[n, t * 8:(t + 1) * 8, :] = total
        for zz in range(NZ):
            e3_out[n, zz] = jnp.concatenate(
                [e3_f[n, pl.ds(zz, CT, stride=8), :], jnp.zeros((16 - CT, 128), F32)], axis=0).astype(BF16)
        for k in order:
            to = lax.rem(z + k, NZ)
            e3_copies.append(remote(e3_out.at[n, to], e3_in.at[n, k], e3s_sem.at[n, k], e3r_sem.at[n, k], z_peer(k)))
    for n in range(NCH):
        total = e3_out[n, z].astype(F32)
        for at, k in enumerate(order):
            e3_copies[n * 7 + at].wait_recv()
            total = total + e3_in[n, k].astype(F32)
        out_ref[n] = total.astype(BF16)

    for copy in list(q_copies.values()) + list(meta_copies.values()) + page_copies + c2_copies + e1_copies + e2_copies + e3_copies:
        copy.wait_send()
    for k in range(GRP):
        for i in range(4):
            if k == 0:
                @pl.when(parity * 4 + i != z)
                def _():
                    part_copy(k, i, z).wait_send()
            else:
                part_copy(k, i, z).wait_send()


def body(queries, lengths, pages, slot_owner, slot_page, value_up, out_proj):
    any_spec = pl.BlockSpec(memory_space=pl.ANY)
    smem = pl.BlockSpec(memory_space=pltpu.SMEM)
    dma = pltpu.SemaphoreType.DMA
    result = pl.pallas_call(
        kernel,
        out_shape=jax.ShapeDtypeStruct((NCH, 16, 128), BF16),
        in_specs=[any_spec, smem, any_spec, smem, smem, any_spec, any_spec],
        out_specs=pl.BlockSpec(memory_space=pltpu.VMEM),
        scratch_shapes=[
            pltpu.VMEM((2, HH, CACHE), BF16),
            pltpu.VMEM((GRP, HH, CACHE), BF16),
            pltpu.VMEM((1, 128), jnp.int32),
            pltpu.VMEM((GRP, 1, 128), jnp.int32),
            pltpu.VMEM((2 * POOL, PAGE, CACHE), BF16),
            pltpu.VMEM((LAT, VDIM), BF16),
            pltpu.VMEM((VDIM, D), BF16),
            pltpu.VMEM((GRP, 4, 16, 384), BF16),
            pltpu.VMEM((GRP, NZ, 16, 384), BF16),
            pltpu.VMEM((4, HEADS, 128), F32),
            pltpu.VMEM((NS, 16, 256), BF16),
            pltpu.VMEM((NS, 16, 256), BF16),
            pltpu.VMEM((NCH, 32, CHUNK), F32),
            pltpu.VMEM((NCH, 32, CHUNK), BF16),
            pltpu.VMEM((NCH, 32, CHUNK), BF16),
            pltpu.VMEM((NCH, NX, 16, CHUNK // 2), BF16),
            pltpu.VMEM((NCH, NX, 16, CHUNK // 2), BF16),
            pltpu.VMEM((NCH, CT * 8, 128), F32),
            pltpu.VMEM((NCH, NZ, 16, 128), BF16),
            pltpu.VMEM((NCH, NZ, 16, 128), BF16),
            dma((6,)), pltpu.SemaphoreType.REGULAR((5,)),
            dma((GRP,)), dma((GRP,)), dma((2,)), dma((2,)), dma((GRP,)), dma((GRP,)),
            dma((GRP, 4)), dma((GRP, NZ)), dma((NS,)), dma((NS,)),
            dma((NCH,)), dma((NCH,)), dma((NCH, NX)), dma((NCH, NX)), dma((NCH, NZ)), dma((NCH, NZ)),
        ],
        compiler_params=pltpu.CompilerParams(
            collective_id=0, has_side_effects=True, vmem_limit_bytes=60 * 1024 * 1024),
    )(queries, lengths, pages, slot_owner, slot_page, value_up, out_proj)
    return result[:, 0:CT].reshape(1, D)


def solution(mesh):
    in_specs = (
        P(("grp", "dev"), None, None),
        P(("grp", "dev")),
        P(("grp", "dev"), None, None),
        P(("grp", "dev")),
        P(("grp", "dev")),
        P("dev", None, None),
        P("dev", None),
    )
    out_specs = P(("grp", "dev"), None)
    return jax.shard_map(body, mesh=mesh, in_specs=in_specs, out_specs=out_specs, check_vma=False)
```

time: 63 us -> 60.7 us (0.963)
  Pallas kernels: 60.8 us -> 58.4 us
    pallas_call x1, Pallas kernels: 60.8 us -> 58.4 us  [body(): pl.pallas_call(kernel, out_shape=jax.ShapeDtypeStruct((NCH, 16, 128), BF1...]
    unnamed x1 -> x0, local copies, waits for them, and re-layouts: 1.34 us -> none
    reshape x0 -> x1, local copies, waits for them, and re-layouts: none -> 1.34 us  [body(): return result[:, 0:CT].reshape(1, D)]
where the time goes in v4:
time: 60.7 us; the launch traced here: 60.4 us
  Pallas kernels  58.4 us (96%)
  local copies, waits for them, and re-layouts  1.34 us (2%)
  between operations  0.66 us (1%)
    pallas_call x1, Pallas kernels, body(): pl.pallas_call(kernel, out_shape=jax.ShapeDtypeStruct((NCH, 16, 128), BF1...  58.4 us
    reshape x1, local copies, waits for them, and re-layouts, body(): return result[:, 0:CT].reshape(1, D)  1.34 us

profile of v4, /device:TPU:1, one launch (start us, length us, event | category | flops | bytes accessed | tf_op | source)
XLA Modules:
  0.0 60.4 jit_solution(12462687521657289176)
XLA Ops:
  0.7 58.4 %shard_map.73 = bf16[4,16,128]{2,1,0:T(8,128)(2,1)} custom-call(bf16[1,64,576]{2,1,0:T(8,128)(2,1)} %q_hbm.1, s32[1]{0:T(128)S(6)} %copy.8.len_ref, bf16[4,64,576]{2,1,0:T(8,128)(2,1)} %pages_hbm.1, s32[4]{0:T(128)} %owner_ref.1, s32[4]{0:T(128)} %page_ref.1, bf16[1,512,128]{2,1,0:T(8,128)(2,1)} %vup_hbm.1, bf16[128,7168]{1,0:T(8,128)(2,1)} %oproj_hbm.1), custom_call_target="tpu_custom_call" | custom-call | tf_op jit(solution)/shard_map/pallas_call | solution.py:313
  59.1 1.3 %reshape.3 = bf16[1,7168]{1,0:T(2,128)(2,1)} reshape(bf16[4,14,128]{2,1,0:T(8,128)(2,1)} %bitcast.1) | data formatting | bytes 28672 | tf_op jit(solution)/shard_map/reshape | solution.py:347

commit v5 on v4

v5 whole, which is shorter than its diff:
```python
import jax
import jax.numpy as jnp
from jax import lax
from jax.experimental import pallas as pl
from jax.experimental.pallas import tpu as pltpu
from jax.sharding import PartitionSpec as P

MESH = pl.DeviceIdType.MESH
F32 = jnp.float32
BF16 = jnp.bfloat16

ROPE = 64
NOPE = 128
SCALE = (NOPE + ROPE) ** -0.5
NEG = -1e30

GRP = 8
NZ = 8
NS = 8
NX = 4
HEADS = 64
LAT = 512
CACHE = 576
HH = HEADS // 2
PAGE = 64
POOL = 4
TOK = 2 * POOL * PAGE
VDIM = 128
D = 7168
HALF = D // 2
TILES = D // 128
NCH = 4
CHUNK = D // NCH
CT = CHUNK // 128


def pieces(value):
    high = value.astype(BF16).astype(F32)
    rest = value - high
    mid = rest.astype(BF16).astype(F32)
    return high, mid, rest - mid


def kernel(q_hbm, len_ref, pages_hbm, owner_ref, page_ref, vup_hbm, oproj_hbm, out_ref,
           q_own, q_in, meta_own, meta_in, pages, vup, oproj, part_out, part_in, stat_out, stat_in,
           lat, c2_out, c2_in, own_f, e1_out, e1_in, e2_out, e2_in, e3_f, e3_out, e3_in,
           loc_sem, in_sem, ms_sem, mr_sem, gs_sem, gr_sem, qs_sem, qr_sem, ps_sem, pr_sem, ts_sem, tr_sem,
           c2s_sem, c2r_sem, e1s_sem, e1r_sem, e2s_sem, e2r_sem, e3s_sem, e3r_sem):
    g = lax.axis_index("grp")
    d = lax.axis_index("dev")
    z = d // NS
    s = d % NS
    x = s // 2
    c = s % 2

    def grp_peer(k):
        return (lax.rem(g + k, GRP), d)

    def z_peer(k):
        return (g, lax.rem(z + k, NZ) * NS + s)

    def s_peer(k):
        return (g, z * NS + lax.rem(s + k, NS))

    barrier = pltpu.get_barrier_semaphore()
    near = [f(k) for f in (grp_peer, z_peer) for k in (1, 7, 2, 6)] + [s_peer(k) for k in range(1, 8)]
    for peer in near:
        pl.semaphore_signal(barrier, inc=1, device_id=peer, device_id_type=MESH)

    q_load = pltpu.make_async_copy(q_hbm.at[0], q_own, loc_sem.at[0])
    q_load.start()
    pages_load = pltpu.make_async_copy(pages_hbm, pages.at[0:POOL], loc_sem.at[1])
    pages_load.start()
    vup_load = pltpu.make_async_copy(vup_hbm.at[0], vup, loc_sem.at[2])
    vup_load.start()
    oproj_load = pltpu.make_async_copy(oproj_hbm, oproj, loc_sem.at[3])
    oproj_load.start()

    lane = lax.broadcasted_iota(jnp.int32, (1, 128), 1)
    meta = jnp.where(lane == 0, len_ref[0], 0)
    for i in range(POOL):
        meta = jnp.where(lane == 1 + i, owner_ref[i], meta)
        meta = jnp.where(lane == 1 + POOL + i, page_ref[i], meta)
    meta_own[...] = meta

    order = (4, 3, 5, 2, 6, 1, 7)

    def tell(sem, peers):
        for peer in peers:
            pl.semaphore_signal(sem, inc=1, device_id=peer, device_id_type=MESH)

    def remote(src, dst, send, recv, peer):
        copy = pltpu.make_async_remote_copy(
            src_ref=src, dst_ref=dst, send_sem=send, recv_sem=recv,
            device_id=peer, device_id_type=MESH)
        copy.start()
        return copy

    def take(ref, sem):
        pltpu.make_async_copy(ref, ref, sem).wait()

    parity = lax.rem(g, 2)
    slots = {1: 0, 7: 1, 2: 2, 6: 3, 4: 4, 3: 5, 5: 6}
    groups = ((1, 7), (2, 6), (4, 3, 5))

    def send_queries(at):
        for k in groups[at]:
            remote(meta_own, meta_in.at[slots[k]], ms_sem.at[0], mr_sem.at[at], grp_peer(k))
            remote(q_hbm.at[0, pl.ds(lax.rem(g + k, 2) * HH, HH)], q_in.at[slots[k]], qs_sem.at[0], qr_sem.at[at], grp_peer(k))

    def take_queries(at):
        first, count = slots[groups[at][0]], len(groups[at])
        take(q_in.at[first:first + count], qr_sem.at[at])

    def take_meta(at):
        first, count = slots[groups[at][0]], len(groups[at])
        take(meta_in.at[first:first + count], mr_sem.at[at])

    pl.semaphore_wait(barrier, 15)
    tell(in_sem.at[0], [grp_peer(2), grp_peer(6)])
    tell(in_sem.at[1], [z_peer(2), z_peer(6)])
    send_queries(0)
    remote(pages_hbm.at[0:2], pages.at[4:6], gs_sem.at[0], gr_sem.at[0], grp_peer(1))
    remote(pages_hbm.at[2:4], pages.at[6:8], gs_sem.at[0], gr_sem.at[0], grp_peer(7))
    send_queries(1)
    pl.semaphore_wait(in_sem.at[0], 2)
    send_queries(2)
    pl.semaphore_wait(in_sem.at[1], 2)
    for at in range(3):
        tell(in_sem.at[2 + at], [grp_peer(k) for k in groups[at]])

    pages_load.wait()
    q_load.wait()
    take_meta(0)
    take(pages.at[4:8], gr_sem.at[0])
    token = lax.broadcasted_iota(jnp.int32, (1, TOK), 1)
    slot = token // PAGE
    owner_v = jnp.zeros((1, TOK), jnp.int32)
    first_v = jnp.zeros((1, TOK), jnp.int32)
    rows = [(meta, i) for i in range(POOL)] + [(meta_in[0], 0), (meta_in[0], 1), (meta_in[1], 2), (meta_in[1], 3)]
    for i, (row, at) in enumerate(rows):
        owner_v = jnp.where(slot == i, row[:, 1 + at:2 + at], owner_v)
        first_v = jnp.where(slot == i, row[:, 1 + POOL + at:2 + POOL + at], first_v)
    pos_v = first_v * PAGE + token % PAGE
    lane64 = lax.broadcasted_iota(jnp.int32, (HEADS, 128), 1)
    lane32 = lax.broadcasted_iota(jnp.int32, (HH, 128), 1)
    row32 = lax.broadcasted_iota(jnp.int32, (HH, 128), 0)

    def partials(members):
        page_all = pages[...].reshape(TOK, CACHE)
        queries, limits, requests = [], [], []
        for k in members:
            row = meta if k == 0 else meta_in[slots[k]]
            queries.append(q_own[pl.ds(parity * HH, HH), :] if k == 0 else q_in[slots[k]])
            limits.append(jnp.broadcast_to(row[:, 0:1], (HH, 1)))
            requests.append(jnp.full((HH, 1), lax.rem(g + (GRP - k), GRP), jnp.int32))
        query = jnp.concatenate(queries, axis=0)
        scores = lax.dot_general(query, page_all, (((1,), (1,)), ((), ())),
                                 preferred_element_type=F32) * SCALE
        live = (pos_v < jnp.concatenate(limits, axis=0)) & (owner_v == jnp.concatenate(requests, axis=0))
        top = jnp.max(jnp.where(live, scores, NEG), axis=1, keepdims=True)
        weights = jnp.where(live, jnp.exp(scores - top), 0.0)
        total = jnp.sum(weights, axis=1, keepdims=True)
        value = jnp.dot(weights.astype(BF16), page_all[:, 0:LAT], preferred_element_type=F32)
        return {k: (top[i * HH:(i + 1) * HH], total[i * HH:(i + 1) * HH], value[i * HH:(i + 1) * HH])
                for i, k in enumerate(members)}

    def send_partial(k, part):
        top, total, value = part
        stat_out[k] = jnp.concatenate(
            [jnp.sum(jnp.where(lane32 == row32, column, 0.0), axis=0, keepdims=True) for column in (top, total)], axis=0)
        for i in range(4):
            rows = slice(i * 8, (i + 1) * 8)
            part_out[k, i] = jnp.concatenate([value[rows, 0:256], value[rows, 256:512]], axis=0).astype(BF16)
        at = min(k, 1)
        for i in range(4):
            zz = parity * 4 + i

            def away():
                peer = (lax.rem(g + (GRP - k), GRP), zz * NS + s)
                remote(stat_out.at[k], stat_in.at[k, z], ts_sem.at[at], tr_sem.at[k], peer)
                remote(part_out.at[k, i], part_in.at[k, z], ps_sem.at[at], pr_sem.at[k], peer)

            if k == 0:
                pl.when(zz != z)(away)

                @pl.when(zz == z)
                def _():
                    pltpu.make_async_copy(stat_out.at[k], stat_in.at[k, z], tr_sem.at[k]).start()
                    pltpu.make_async_copy(part_out.at[k, i], part_in.at[k, z], pr_sem.at[k]).start()
            else:
                away()

    for at, members in enumerate(((1, 7, 0), (2, 6), (4, 3, 5))):
        if at:
            take_meta(at)
        take_queries(at)
        done = partials(members)
        pl.semaphore_wait(in_sem.at[2 + at], len(groups[at]))
        for k in members:
            send_partial(k, done[k])

    odd = lax.rem(g + z // 4, 2)
    sources = [even_k + odd * (odd_k - even_k) for even_k, odd_k in ((0, 1), (2, 7), (6, 3), (4, 5))]
    mine = lane64 == lax.rem(z, 4) * 8 + lax.broadcasted_iota(jnp.int32, (HEADS, 128), 0) % 8
    tops, totals = [], []
    for k in sources:
        take(stat_in.at[k], tr_sem.at[k])
        take(part_in.at[k], pr_sem.at[k])
        for at, columns in enumerate((tops, totals)):
            spread = jnp.broadcast_to(stat_in[k, :, at:at + 1, :], (NZ, 8, 128)).reshape(HEADS, 128)
            columns.append(jnp.sum(jnp.where(mine, spread, 0.0), axis=1, keepdims=True))
    best = tops[0]
    for top in tops[1:]:
        best = jnp.maximum(best, top)
    factors = [jnp.exp(top - best) for top in tops]
    denominator = 0.0
    for factor, total in zip(factors, totals):
        denominator = denominator + factor * total
    scale = 1.0 / denominator
    factors = [factor * scale for factor in factors]
    for j in range(4):
        block = 0.0
        for k, factor in zip(sources, factors):
            both = part_in[k, :, :, j % 2 * 128:j % 2 * 128 + 128].astype(F32)
            block = block + factor * both[:, j // 2 * 8:j // 2 * 8 + 8].reshape(HEADS, 128)
        lat[j] = block

    for ss in range(NS):
        quarters = [lat[j, pl.ds(ss, NZ, stride=NS), :] for j in range(4)]
        c2_out[ss] = jnp.concatenate([jnp.concatenate(quarters[0:2], axis=1), jnp.concatenate(quarters[2:4], axis=1)], axis=0).astype(BF16)
    for k in order:
        remote(c2_out.at[lax.rem(s + k, NS)], c2_in.at[s], c2s_sem.at[0], c2r_sem.at[0], s_peer(k))
    pltpu.make_async_copy(c2_out.at[s], c2_in.at[s], c2r_sem.at[0]).start()
    vup_load.wait()
    take(c2_in, c2r_sem.at[0])

    blocks = []
    for dc in (1, 0):
        for dx in range(NX):
            at = lax.rem(x + dx, NX) * 2 + lax.rem(c + dc, 2)
            both = c2_in[at].astype(F32)
            blocks.append(jnp.concatenate([both[0:8, :], both[8:16, :]], axis=1))
    heads_in = jnp.concatenate(blocks, axis=0).astype(BF16)
    head_value = jnp.dot(heads_in, vup[...], preferred_element_type=F32).astype(BF16)

    oproj_load.wait()
    core_peer = (g, z * NS + x * 2 + (1 - c))
    for n in range(NCH):
        cols = slice(n * CHUNK, (n + 1) * CHUNK)
        product = jnp.dot(head_value, oproj[:, cols], preferred_element_type=F32)
        e1_out[n] = product[0:32].astype(BF16)
        remote(e1_out.at[n], e1_in.at[n], e1s_sem.at[0], e1r_sem.at[n], core_peer)
        own_f[n] = product[32:64]

    for n in range(NCH):
        take(e1_in.at[n], e1r_sem.at[n])
        both = own_f[n] + e1_in[n].astype(F32)
        own_f[n] = both
        for dx in (2, 1, 3):
            rows = both[dx * 8:(dx + 1) * 8]
            e2_out[n, dx] = jnp.concatenate([rows[:, 0:CHUNK // 2], rows[:, CHUNK // 2:CHUNK]], axis=0).astype(BF16)
            peer = (g, z * NS + lax.rem(x + dx, NX) * 2 + c)
            remote(e2_out.at[n, dx], e2_in.at[n, dx], e2s_sem.at[0], e2r_sem.at[n], peer)

    for n in range(NCH):
        take(e2_in.at[n, 1:NX], e2r_sem.at[n])
        for t in range(CT):
            half, col = t // (CT // 2), t % (CT // 2) * 128
            total = own_f[n, 0:8, t * 128:(t + 1) * 128]
            for dx in (1, 3, 2):
                total = total + e2_in[n, dx, :, col:col + 128].astype(F32)[half * 8:half * 8 + 8]
            e3_f[n, t * 8:(t + 1) * 8, :] = total
        for zz in range(NZ):
            e3_out[n, zz] = jnp.concatenate(
                [e3_f[n, pl.ds(zz, CT, stride=8), :], jnp.zeros((16 - CT, 128), F32)], axis=0).astype(BF16)
        for k in order:
            to = lax.rem(z + k, NZ)
            remote(e3_out.at[n, to], e3_in.at[n, k], e3s_sem.at[0], e3r_sem.at[n], z_peer(k))
    for n in range(NCH):
        take(e3_in.at[n, 1:NZ], e3r_sem.at[n])
        total = e3_out[n, z].astype(F32)
        for k in order:
            total = total + e3_in[n, k].astype(F32)
        out_ref[n] = total.astype(BF16)

    take(q_in.at[0:7], qs_sem.at[0])
    take(meta_in.at[0:7], ms_sem.at[0])
    take(pages.at[4:8], gs_sem.at[0])
    take(part_out.at[1:GRP], ps_sem.at[1])
    take(stat_in.at[1:GRP, 0:4], ts_sem.at[1])

    @pl.when(z // 4 == parity)
    def _():
        take(part_out.at[0, 0:3], ps_sem.at[0])
        take(stat_in.at[0, 0:3], ts_sem.at[0])

    @pl.when(z // 4 != parity)
    def _():
        take(part_out.at[0], ps_sem.at[0])
        take(stat_in.at[0, 0:4], ts_sem.at[0])

    take(c2_out.at[1:NS], c2s_sem.at[0])
    take(e1_out, e1s_sem.at[0])
    take(e2_out.at[:, 1:NX], e2s_sem.at[0])
    take(e3_out.at[:, 1:NZ], e3s_sem.at[0])


def body(queries, lengths, pages, slot_owner, slot_page, value_up, out_proj):
    any_spec = pl.BlockSpec(memory_space=pl.ANY)
    smem = pl.BlockSpec(memory_space=pltpu.SMEM)
    dma = pltpu.SemaphoreType.DMA
    result = pl.pallas_call(
        kernel,
        out_shape=jax.ShapeDtypeStruct((NCH, 16, 128), BF16),
        in_specs=[any_spec, smem, any_spec, smem, smem, any_spec, any_spec],
        out_specs=pl.BlockSpec(memory_space=pltpu.VMEM),
        scratch_shapes=[
            pltpu.VMEM((HEADS, CACHE), BF16),
            pltpu.VMEM((GRP, HH, CACHE), BF16),
            pltpu.VMEM((1, 128), jnp.int32),
            pltpu.VMEM((GRP, 1, 128), jnp.int32),
            pltpu.VMEM((2 * POOL, PAGE, CACHE), BF16),
            pltpu.VMEM((LAT, VDIM), BF16),
            pltpu.VMEM((VDIM, D), BF16),
            pltpu.VMEM((GRP, 4, 16, 256), BF16),
            pltpu.VMEM((GRP, NZ, 16, 256), BF16),
            pltpu.VMEM((GRP, 2, 128), F32),
            pltpu.VMEM((GRP, NZ, 2, 128), F32),
            pltpu.VMEM((4, HEADS, 128), F32),
            pltpu.VMEM((NS, 16, 256), BF16),
            pltpu.VMEM((NS, 16, 256), BF16),
            pltpu.VMEM((NCH, 32, CHUNK), F32),
            pltpu.VMEM((NCH, 32, CHUNK), BF16),
            pltpu.VMEM((NCH, 32, CHUNK), BF16),
            pltpu.VMEM((NCH, NX, 16, CHUNK // 2), BF16),
            pltpu.VMEM((NCH, NX, 16, CHUNK // 2), BF16),
            pltpu.VMEM((NCH, CT * 8, 128), F32),
            pltpu.VMEM((NCH, NZ, 16, 128), BF16),
            pltpu.VMEM((NCH, NZ, 16, 128), BF16),
            dma((4,)), pltpu.SemaphoreType.REGULAR((5,)),
            dma((1,)), dma((3,)), dma((1,)), dma((1,)), dma((1,)), dma((3,)),
            dma((2,)), dma((GRP,)), dma((2,)), dma((GRP,)), dma((1,)), dma((1,)),
            dma((1,)), dma((NCH,)), dma((1,)), dma((NCH,)), dma((1,)), dma((NCH,)),
        ],
        compiler_params=pltpu.CompilerParams(
            collective_id=0, has_side_effects=True, vmem_limit_bytes=60 * 1024 * 1024),
    )(queries, lengths, pages, slot_owner, slot_page, value_up, out_proj)
    return result[:, 0:CT].reshape(1, D)


def solution(mesh):
    in_specs = (
        P(("grp", "dev"), None, None),
        P(("grp", "dev")),
        P(("grp", "dev"), None, None),
        P(("grp", "dev")),
        P(("grp", "dev")),
        P("dev", None, None),
        P("dev", None),
    )
    out_specs = P(("grp", "dev"), None)
    return jax.shard_map(body, mesh=mesh, in_specs=in_specs, out_specs=out_specs, check_vma=False)
```

time: 60.7 us -> 57.6 us (0.949)
  Pallas kernels: 58.4 us -> 55.4 us
    pallas_call x1, Pallas kernels: 58.4 us -> 55.4 us  [body(): pl.pallas_call(kernel, out_shape=jax.ShapeDtypeStruct((NCH, 16, 128), BF1...]
where the time goes in v5:
time: 57.6 us; the launch traced here: 57.4 us
  Pallas kernels  55.4 us (96%)
  local copies, waits for them, and re-layouts  1.34 us (2%)
  between operations  0.66 us (1%)
    pallas_call x1, Pallas kernels, body(): pl.pallas_call(kernel, out_shape=jax.ShapeDtypeStruct((NCH, 16, 128), BF1...  55.4 us
    reshape x1, local copies, waits for them, and re-layouts, body(): return result[:, 0:CT].reshape(1, D)  1.34 us

profile of v5, /device:TPU:1, one launch (start us, length us, event | category | flops | bytes accessed | tf_op | source)
XLA Modules:
  0.0 57.4 jit_solution(14609103123212065600)
XLA Ops:
  0.7 55.4 %shard_map.73 = bf16[4,16,128]{2,1,0:T(8,128)(2,1)} custom-call(bf16[1,64,576]{2,1,0:T(8,128)(2,1)} %q_hbm.1, s32[1]{0:T(128)S(6)} %copy.8.len_ref, bf16[4,64,576]{2,1,0:T(8,128)(2,1)} %pages_hbm.1, s32[4]{0:T(128)} %owner_ref.1, s32[4]{0:T(128)} %page_ref.1, bf16[1,512,128]{2,1,0:T(8,128)(2,1)} %vup_hbm.1, bf16[128,7168]{1,0:T(8,128)(2,1)} %oproj_hbm.1), custom_call_target="tpu_custom_call" | custom-call | tf_op jit(solution)/shard_map/pallas_call | solution.py:313
  56.1 1.3 %reshape.3 = bf16[1,7168]{1,0:T(2,128)(2,1)} reshape(bf16[4,14,128]{2,1,0:T(8,128)(2,1)} %bitcast.1) | data formatting | bytes 28672 | tf_op jit(solution)/shard_map/reshape | solution.py:349

commit v6 on v5

--- a/solution.py
+++ b/solution.py
@@ -41,10 +41,10 @@
     return high, mid, rest - mid
 
 
-def kernel(q_hbm, len_ref, pages_hbm, owner_ref, page_ref, vup_hbm, oproj_hbm, out_ref,
-           q_own, q_in, meta_own, meta_in, pages, vup, oproj, part_out, part_in, stat_out, stat_in,
-           lat, c2_out, c2_in, own_f, e1_out, e1_in, e2_out, e2_in, e3_f, e3_out, e3_in,
-           loc_sem, in_sem, ms_sem, mr_sem, gs_sem, gr_sem, qs_sem, qr_sem, ps_sem, pr_sem, ts_sem, tr_sem,
+def kernel(q_hbm, len_hbm, pages_hbm, owner_hbm, page_hbm, vup_hbm, oproj_hbm, out_ref,
+           len_ref, owner_ref, page_ref, q_own, q_in, rope_own, rope_in, prope_out, prope_in, meta_own, meta_in, pages, vup, oproj, part_out, part_in, stat_out, stat_in,
+           row_f, lat, c2_out, c2_in, own_f, e1_out, e1_in, e2_out, e2_in, e3_f, e3_out, e3_in,
+           loc_sem, in_sem, ms_sem, mr_sem, gs_sem, gr_sem, qs_sem, qr_sem, rs_sem, rr_sem, ps_sem, pr_sem, ts_sem, tr_sem,
            c2s_sem, c2r_sem, e1s_sem, e1r_sem, e2s_sem, e2r_sem, e3s_sem, e3r_sem):
     g = lax.axis_index("grp")
     d = lax.axis_index("dev")
@@ -69,6 +69,10 @@
 
     q_load = pltpu.make_async_copy(q_hbm.at[0], q_own, loc_sem.at[0])
     q_load.start()
+    number_loads = [pltpu.make_async_copy(src, dst, loc_sem.at[4 + at]) for at, (src, dst) in
+                    enumerate(((len_hbm, len_ref), (owner_hbm, owner_ref), (page_hbm, page_ref)))]
+    for load in number_loads:
+        load.start()
     pages_load = pltpu.make_async_copy(pages_hbm, pages.at[0:POOL], loc_sem.at[1])
     pages_load.start()
     vup_load = pltpu.make_async_copy(vup_hbm.at[0], vup, loc_sem.at[2])
@@ -76,63 +80,85 @@
     oproj_load = pltpu.make_async_copy(oproj_hbm, oproj, loc_sem.at[3])
     oproj_load.start()
 
+    def tell(sem, peers):
+        for peer in peers:
+            pl.semaphore_signal(sem, inc=1, device_id=peer, device_id_type=MESH)
+
+    def remote(src, dst, send, recv, peer):
+        copy = pltpu.make_async_remote_copy(
+            src_ref=src, dst_ref=dst, send_sem=send, recv_sem=recv,
+            device_id=peer, device_id_type=MESH)
+        copy.start()
+        return copy
+
+    def take(ref, sem):
+        pltpu.make_async_copy(ref, ref, sem).wait()
+
+    parity = lax.rem(g, 2)
+    slots = {1: 0, 7: 1, 2: 2, 6: 3, 4: 4, 3: 5, 5: 6}
+    groups = ((1, 7), (2, 6), (4, 3, 5))
+
+    def send_queries(at):
+        for k in groups[at]:
+            remote(q_hbm.at[0, pl.ds(lax.rem(g + k, 2) * HH, HH), 0:LAT], q_in.at[slots[k]], qs_sem.at[0], qr_sem.at[at], grp_peer(k))
+
+    def send_sides(at):
+        for k in groups[at]:
+            remote(meta_own, meta_in.at[slots[k]], ms_sem.at[0], mr_sem.at[at], grp_peer(k))
+            remote(rope_own.at[lax.rem(g + k, 2)], rope_in.at[slots[k]], rs_sem.at[0], rr_sem.at[at], grp_peer(k))
+
+    def take_queries(at):
+        first, count = slots[groups[at][0]], len(groups[at])
+        take(rope_in.at[first:first + count], rr_sem.at[at])
+        take(q_in.at[first:first + count], qr_sem.at[at])
+
+    def take_meta(at):
+        first, count = slots[groups[at][0]], len(groups[at])
+        take(meta_in.at[first:first + count], mr_sem.at[at])
+
+    pl.semaphore_wait(barrier, 15)
+    tell(in_sem.at[0], [grp_peer(2), grp_peer(6)])
+    tell(in_sem.at[1], [z_peer(2), z_peer(6)])
+    send_queries(0)
+    send_queries(1)
+    remote(pages_hbm.at[0:2, :, 0:LAT], pages.at[4:6, :, 0:LAT], gs_sem.at[0], gr_sem.at[0], grp_peer(1))
+    remote(pages_hbm.at[2:4, :, 0:LAT], pages.at[6:8, :, 0:LAT], gs_sem.at[0], gr_sem.at[0], grp_peer(7))
+
+    for load in number_loads:
+        load.wait()
     lane = lax.broadcasted_iota(jnp.int32, (1, 128), 1)
     meta = jnp.where(lane == 0, len_ref[0], 0)
     for i in range(POOL):
         meta = jnp.where(lane == 1 + i, owner_ref[i], meta)
         meta = jnp.where(lane == 1 + POOL + i, page_ref[i], meta)
     meta_own[...] = meta
-
-    order = (4, 3, 5, 2, 6, 1, 7)
-
-    def tell(sem, peers):
-        for peer in peers:
-            pl.semaphore_signal(sem, inc=1, device_id=peer, device_id_type=MESH)
-
-    def remote(src, dst, send, recv, peer):
-        copy = pltpu.make_async_remote_copy(
-            src_ref=src, dst_ref=dst, send_sem=send, recv_sem=recv,
-            device_id=peer, device_id_type=MESH)
-        copy.start()
-        return copy
-
-    def take(ref, sem):
-        pltpu.make_async_copy(ref, ref, sem).wait()
-
-    parity = lax.rem(g, 2)
-    slots = {1: 0, 7: 1, 2: 2, 6: 3, 4: 4, 3: 5, 5: 6}
-    groups = ((1, 7), (2, 6), (4, 3, 5))
-
-    def send_queries(at):
-        for k in groups[at]:
-            remote(meta_own, meta_in.at[slots[k]], ms_sem.at[0], mr_sem.at[at], grp_peer(k))
-            remote(q_hbm.at[0, pl.ds(lax.rem(g + k, 2) * HH, HH)], q_in.at[slots[k]], qs_sem.at[0], qr_sem.at[at], grp_peer(k))
-
-    def take_queries(at):
-        first, count = slots[groups[at][0]], len(groups[at])
-        take(q_in.at[first:first + count], qr_sem.at[at])
-
-    def take_meta(at):
-        first, count = slots[groups[at][0]], len(groups[at])
-        take(meta_in.at[first:first + count], mr_sem.at[at])
-
-    pl.semaphore_wait(barrier, 15)
-    tell(in_sem.at[0], [grp_peer(2), grp_peer(6)])
-    tell(in_sem.at[1], [z_peer(2), z_peer(6)])
-    send_queries(0)
-    remote(pages_hbm.at[0:2], pages.at[4:6], gs_sem.at[0], gr_sem.at[0], grp_peer(1))
-    remote(pages_hbm.at[2:4], pages.at[6:8], gs_sem.at[0], gr_sem.at[0], grp_peer(7))
-    send_queries(1)
+    q_load.wait()
+    for half in range(2):
+        rope = q_own[half * HH:(half + 1) * HH, LAT:CACHE].astype(F32)
+        rope_own[half] = jnp.concatenate([rope[0:16], rope[16:32]], axis=1).astype(BF16)
+    send_sides(0)
+    pages_load.wait()
+    for side in range(2):
+        rope = [pages[2 * side + i, :, LAT:CACHE].astype(F32) for i in range(2)]
+        prope_out[side] = jnp.concatenate(rope, axis=1).astype(BF16)
+    remote(prope_out.at[0], prope_in.at[0], gs_sem.at[1], gr_sem.at[1], grp_peer(1))
+    remote(prope_out.at[1], prope_in.at[1], gs_sem.at[1], gr_sem.at[1], grp_peer(7))
+    send_sides(1)
     pl.semaphore_wait(in_sem.at[0], 2)
     send_queries(2)
+    send_sides(2)
     pl.semaphore_wait(in_sem.at[1], 2)
     for at in range(3):
         tell(in_sem.at[2 + at], [grp_peer(k) for k in groups[at]])
 
-    pages_load.wait()
-    q_load.wait()
+    order = (4, 3, 5, 2, 6, 1, 7)
     take_meta(0)
-    take(pages.at[4:8], gr_sem.at[0])
+    take(prope_in, gr_sem.at[1])
+    take(pages.at[4:8, :, 0:LAT], gr_sem.at[0])
+    for side in range(2):
+        rope = prope_in[side].astype(F32)
+        for i in range(2):
+            pages[4 + 2 * side + i, :, LAT:CACHE] = rope[:, i * ROPE:(i + 1) * ROPE].astype(BF16)
     token = lax.broadcasted_iota(jnp.int32, (1, TOK), 1)
     slot = token // PAGE
     owner_v = jnp.zeros((1, TOK), jnp.int32)
@@ -151,7 +177,12 @@
         queries, limits, requests = [], [], []
         for k in members:
             row = meta if k == 0 else meta_in[slots[k]]
-            queries.append(q_own[pl.ds(parity * HH, HH), :] if k == 0 else q_in[slots[k]])
+            if k == 0:
+                queries.append(q_own[pl.ds(parity * HH, HH), :])
+            else:
+                rope = rope_in[slots[k]].astype(F32)
+                rope = jnp.concatenate([rope[:, 0:ROPE], rope[:, ROPE:2 * ROPE]], axis=0).astype(BF16)
+                queries.append(jnp.concatenate([q_in[slots[k]], rope], axis=1))
             limits.append(jnp.broadcast_to(row[:, 0:1], (HH, 1)))
             requests.append(jnp.full((HH, 1), lax.rem(g + (GRP - k), GRP), jnp.int32))
         query = jnp.concatenate(queries, axis=0)
@@ -282,11 +313,15 @@
         total = e3_out[n, z].astype(F32)
         for k in order:
             total = total + e3_in[n, k].astype(F32)
-        out_ref[n] = total.astype(BF16)
+        for t in range(CT):
+            row_f[:, n * CHUNK + t * 128:n * CHUNK + (t + 1) * 128] = total[t:t + 1]
+    out_ref[...] = row_f[...].astype(BF16)
 
     take(q_in.at[0:7], qs_sem.at[0])
     take(meta_in.at[0:7], ms_sem.at[0])
-    take(pages.at[4:8], gs_sem.at[0])
+    take(rope_in.at[0:7], rs_sem.at[0])
+    take(pages.at[4:8, :, 0:LAT], gs_sem.at[0])
+    take(prope_out, gs_sem.at[1])
     take(part_out.at[1:GRP], ps_sem.at[1])
     take(stat_in.at[1:GRP, 0:4], ts_sem.at[1])
 
@@ -308,16 +343,22 @@
 
 def body(queries, lengths, pages, slot_owner, slot_page, value_up, out_proj):
     any_spec = pl.BlockSpec(memory_space=pl.ANY)
-    smem = pl.BlockSpec(memory_space=pltpu.SMEM)
     dma = pltpu.SemaphoreType.DMA
-    result = pl.pallas_call(
+    return pl.pallas_call(
         kernel,
-        out_shape=jax.ShapeDtypeStruct((NCH, 16, 128), BF16),
-        in_specs=[any_spec, smem, any_spec, smem, smem, any_spec, any_spec],
+        out_shape=jax.ShapeDtypeStruct((1, D), BF16),
+        in_specs=[any_spec] * 7,
         out_specs=pl.BlockSpec(memory_space=pltpu.VMEM),
         scratch_shapes=[
+            pltpu.SMEM((1,), jnp.int32),
+            pltpu.SMEM((POOL,), jnp.int32),
+            pltpu.SMEM((POOL,), jnp.int32),
             pltpu.VMEM((HEADS, CACHE), BF16),
-            pltpu.VMEM((GRP, HH, CACHE), BF16),
+            pltpu.VMEM((GRP, HH, LAT), BF16),
+            pltpu.VMEM((2, 16, 128), BF16),
+            pltpu.VMEM((GRP, 16, 128), BF16),
+            pltpu.VMEM((2, PAGE, 128), BF16),
+            pltpu.VMEM((2, PAGE, 128), BF16),
             pltpu.VMEM((1, 128), jnp.int32),
             pltpu.VMEM((GRP, 1, 128), jnp.int32),
             pltpu.VMEM((2 * POOL, PAGE, CACHE), BF16),
@@ -327,6 +368,7 @@
             pltpu.VMEM((GRP, NZ, 16, 256), BF16),
             pltpu.VMEM((GRP, 2, 128), F32),
             pltpu.VMEM((GRP, NZ, 2, 128), F32),
+            pltpu.VMEM((1, D), F32),
             pltpu.VMEM((4, HEADS, 128), F32),
             pltpu.VMEM((NS, 16, 256), BF16),
             pltpu.VMEM((NS, 16, 256), BF16),
@@ -338,15 +380,14 @@
             pltpu.VMEM((NCH, CT * 8, 128), F32),
             pltpu.VMEM((NCH, NZ, 16, 128), BF16),
             pltpu.VMEM((NCH, NZ, 16, 128), BF16),
-            dma((4,)), pltpu.SemaphoreType.REGULAR((5,)),
-            dma((1,)), dma((3,)), dma((1,)), dma((1,)), dma((1,)), dma((3,)),
+            dma((7,)), pltpu.SemaphoreType.REGULAR((5,)),
+            dma((1,)), dma((3,)), dma((2,)), dma((2,)), dma((1,)), dma((3,)), dma((1,)), dma((3,)),
             dma((2,)), dma((GRP,)), dma((2,)), dma((GRP,)), dma((1,)), dma((1,)),
             dma((1,)), dma((NCH,)), dma((1,)), dma((NCH,)), dma((1,)), dma((NCH,)),
         ],
         compiler_params=pltpu.CompilerParams(
             collective_id=0, has_side_effects=True, vmem_limit_bytes=60 * 1024 * 1024),
     )(queries, lengths, pages, slot_owner, slot_page, value_up, out_proj)
-    return result[:, 0:CT].reshape(1, D)
 
 
 def solution(mesh):

time: 57.6 us -> 56.2 us (0.976)
  Pallas kernels: 55.4 us -> 54 us
    pallas_call x1, Pallas kernels: 55.4 us -> 54 us  [body(): pl.pallas_call(kernel, out_shape=jax.ShapeDtypeStruct((1, D), BF16), in_s...]
    unnamed x0 -> x1, local copies, waits for them, and re-layouts: none -> 1.39 us
    reshape x1 -> x0, local copies, waits for them, and re-layouts: 1.34 us -> none  [body(): return result[:, 0:CT].reshape(1, D)]
where the time goes in v6:
time: 56.2 us; the launch traced here: 56 us
  Pallas kernels  54 us (96%)
  local copies, waits for them, and re-layouts  1.39 us (2%)
  between operations  0.66 us (1%)
    pallas_call x1, Pallas kernels, body(): pl.pallas_call(kernel, out_shape=jax.ShapeDtypeStruct((1, D), BF16), in_s...  54 us
    unnamed x1, local copies, waits for them, and re-layouts  1.39 us

profile of v6, /device:TPU:1, one launch (start us, length us, event | category | flops | bytes accessed | tf_op | source)
XLA Modules:
  0.0 56.0 jit_solution(12554196543399662766)
XLA Ops:
  0.7 54.0 %shard_map.73 = bf16[1,7168]{1,0:T(2,128)(2,1)} custom-call(bf16[1,64,576]{2,1,0:T(8,128)(2,1)} %q_hbm.1, s32[1]{0:T(128)S(6)} %copy.9.len_hbm, bf16[4,64,576]{2,1,0:T(8,128)(2,1)} %pages_hbm.1, s32[4]{0:T(128)} %owner_hbm.1, s32[4]{0:T(128)} %page_hbm.1, bf16[1,512,128]{2,1,0:T(8,128)(2,1)} %vup_hbm.1, bf16[128,7168]{1,0:T(8,128)(2,1)} %oproj_hbm.1), custom_call_target="tpu_custom_call" | custom-call | tf_op jit(solution)/shard_map/pallas_call | solution.py:347
  54.7 1.4 %copy.10 = bf16[1,7168]{1,0:T(2,128)(2,1)} copy(bf16[1,7168]{1,0:T(2,128)(2,1)} %shard_map.73) | data formatting | bytes 28672

commit v7 on v6

--- a/solution.py
+++ b/solution.py
@@ -30,6 +30,7 @@
 HALF = D // 2
 TILES = D // 128
 NCH = 4
+NX1 = 3
 CHUNK = D // NCH
 CT = CHUNK // 128
 
@@ -43,9 +44,9 @@
 
 def kernel(q_hbm, len_hbm, pages_hbm, owner_hbm, page_hbm, vup_hbm, oproj_hbm, out_ref,
            len_ref, owner_ref, page_ref, q_own, q_in, rope_own, rope_in, prope_out, prope_in, meta_own, meta_in, pages, vup, oproj, part_out, part_in, stat_out, stat_in,
-           row_f, lat, c2_out, c2_in, own_f, e1_out, e1_in, e2_out, e2_in, e3_f, e3_out, e3_in,
+           row_f, lat, c2_out, c2_in, own_f, e1_out, e1_in, e2_out, e2_in, e3_f, e3_out, e3_in, f1_f, f1_out, f1_in, f2_f, f2_out, f2_in,
            loc_sem, in_sem, ms_sem, mr_sem, gs_sem, gr_sem, qs_sem, qr_sem, rs_sem, rr_sem, ps_sem, pr_sem, ts_sem, tr_sem,
-           c2s_sem, c2r_sem, e1s_sem, e1r_sem, e2s_sem, e2r_sem, e3s_sem, e3r_sem):
+           c2s_sem, c2r_sem, e1s_sem, e1r_sem, e2s_sem, e2r_sem, e3s_sem, e3r_sem, f1s_sem, f1r_sem, f2s_sem, f2r_sem):
     g = lax.axis_index("grp")
     d = lax.axis_index("dev")
     z = d // NS
@@ -95,12 +96,12 @@
         pltpu.make_async_copy(ref, ref, sem).wait()
 
     parity = lax.rem(g, 2)
-    slots = {1: 0, 7: 1, 2: 2, 6: 3, 4: 4, 3: 5, 5: 6}
-    groups = ((1, 7), (2, 6), (4, 3, 5))
+    slots = {1: 0, 7: 1, 2: 2, 6: 3, 3: 4, 5: 5, 4: 6}
+    groups = ((1, 7), (2, 6), (3, 5, 4))
 
     def send_queries(at):
         for k in groups[at]:
-            remote(q_hbm.at[0, pl.ds(lax.rem(g + k, 2) * HH, HH), 0:LAT], q_in.at[slots[k]], qs_sem.at[0], qr_sem.at[at], grp_peer(k))
+            remote(q_own.at[pl.ds(lax.rem(g + k, 2) * HH, HH), 0:LAT], q_in.at[slots[k]], qs_sem.at[0], qr_sem.at[at], grp_peer(k))
 
     def send_sides(at):
         for k in groups[at]:
@@ -116,14 +117,8 @@
         first, count = slots[groups[at][0]], len(groups[at])
         take(meta_in.at[first:first + count], mr_sem.at[at])
 
-    pl.semaphore_wait(barrier, 15)
-    tell(in_sem.at[0], [grp_peer(2), grp_peer(6)])
-    tell(in_sem.at[1], [z_peer(2), z_peer(6)])
-    send_queries(0)
-    send_queries(1)
-    remote(pages_hbm.at[0:2, :, 0:LAT], pages.at[4:6, :, 0:LAT], gs_sem.at[0], gr_sem.at[0], grp_peer(1))
-    remote(pages_hbm.at[2:4, :, 0:LAT], pages.at[6:8, :, 0:LAT], gs_sem.at[0], gr_sem.at[0], grp_peer(7))
-
+    q_load.wait()
+    pages_load.wait()
     for load in number_loads:
         load.wait()
     lane = lax.broadcasted_iota(jnp.int32, (1, 128), 1)
@@ -132,15 +127,21 @@
         meta = jnp.where(lane == 1 + i, owner_ref[i], meta)
         meta = jnp.where(lane == 1 + POOL + i, page_ref[i], meta)
     meta_own[...] = meta
-    q_load.wait()
     for half in range(2):
         rope = q_own[half * HH:(half + 1) * HH, LAT:CACHE].astype(F32)
         rope_own[half] = jnp.concatenate([rope[0:16], rope[16:32]], axis=1).astype(BF16)
-    send_sides(0)
-    pages_load.wait()
     for side in range(2):
         rope = [pages[2 * side + i, :, LAT:CACHE].astype(F32) for i in range(2)]
         prope_out[side] = jnp.concatenate(rope, axis=1).astype(BF16)
+    pl.semaphore_wait(barrier, 15)
+    tell(in_sem.at[0], [grp_peer(2), grp_peer(6)])
+    tell(in_sem.at[1], [z_peer(2), z_peer(6)])
+    send_queries(0)
+    send_queries(1)
+    remote(pages.at[0:2, :, 0:LAT], pages.at[4:6, :, 0:LAT], gs_sem.at[0], gr_sem.at[0], grp_peer(1))
+    remote(pages.at[2:4, :, 0:LAT], pages.at[6:8, :, 0:LAT], gs_sem.at[0], gr_sem.at[0], grp_peer(7))
+
+    send_sides(0)
     remote(prope_out.at[0], prope_in.at[0], gs_sem.at[1], gr_sem.at[1], grp_peer(1))
     remote(prope_out.at[1], prope_in.at[1], gs_sem.at[1], gr_sem.at[1], grp_peer(7))
     send_sides(1)
@@ -222,7 +223,7 @@
             else:
                 away()
 
-    for at, members in enumerate(((1, 7, 0), (2, 6), (4, 3, 5))):
+    for at, members in enumerate(((1, 7, 0), (2, 6), (3, 5, 4))):
         if at:
             take_meta(at)
         take_queries(at)
@@ -277,14 +278,24 @@
 
     oproj_load.wait()
     core_peer = (g, z * NS + x * 2 + (1 - c))
-    for n in range(NCH):
+    for n in (NX1, 0, 1, 2):
         cols = slice(n * CHUNK, (n + 1) * CHUNK)
         product = jnp.dot(head_value, oproj[:, cols], preferred_element_type=F32)
         e1_out[n] = product[0:32].astype(BF16)
         remote(e1_out.at[n], e1_in.at[n], e1s_sem.at[0], e1r_sem.at[n], core_peer)
         own_f[n] = product[32:64]
 
-    for n in range(NCH):
+    take(e1_in.at[NX1], e1r_sem.at[NX1])
+    both = own_f[NX1] + e1_in[NX1].astype(F32)
+    for t in range(CT):
+        f1_f[t * 32:(t + 1) * 32, :] = both[:, t * 128:(t + 1) * 128]
+    f1_f[CT * 32:512, :] = jnp.zeros((512 - CT * 32, 128), F32)
+    for zz in range(NZ):
+        f1_out[zz] = f1_f[pl.ds(zz, 64, stride=8), :].astype(BF16)
+    for k in order:
+        remote(f1_out.at[lax.rem(z + k, NZ)], f1_in.at[k], f1s_sem.at[0], f1r_sem.at[0], z_peer(k))
+
+    for n in range(NX1):
         take(e1_in.at[n], e1r_sem.at[n])
         both = own_f[n] + e1_in[n].astype(F32)
         own_f[n] = both
@@ -294,7 +305,7 @@
             peer = (g, z * NS + lax.rem(x + dx, NX) * 2 + c)
             remote(e2_out.at[n, dx], e2_in.at[n, dx], e2s_sem.at[0], e2r_sem.at[n], peer)
 
-    for n in range(NCH):
+    for n in range(NX1):
         take(e2_in.at[n, 1:NX], e2r_sem.at[n])
         for t in range(CT):
             half, col = t // (CT // 2), t % (CT // 2) * 128
@@ -308,13 +319,33 @@
         for k in order:
             to = lax.rem(z + k, NZ)
             remote(e3_out.at[n, to], e3_in.at[n, k], e3s_sem.at[0], e3r_sem.at[n], z_peer(k))
-    for n in range(NCH):
+
+    take(f1_in.at[1:NZ], f1r_sem.at[0])
+    total = f1_out[z].astype(F32)
+    for k in order:
+        total = total + f1_in[k].astype(F32)
+    f2_f[...] = total
+    for dx in (2, 1, 3):
+        f2_out[dx] = f2_f[pl.ds(dx, 16, stride=4), :].astype(BF16)
+        peer = (g, z * NS + lax.rem(x + dx, NX) * 2 + c)
+        remote(f2_out.at[dx], f2_in.at[dx], f2s_sem.at[0], f2r_sem.at[0], peer)
+    f2_own = f2_f[pl.ds(0, 16, stride=4), :]
+
+    def put(n, total):
+        for t in range(CT):
+            row_f[:, n * CHUNK + t * 128:n * CHUNK + (t + 1) * 128] = total[t:t + 1]
+
+    for n in range(NX1):
         take(e3_in.at[n, 1:NZ], e3r_sem.at[n])
         total = e3_out[n, z].astype(F32)
         for k in order:
             total = total + e3_in[n, k].astype(F32)
-        for t in range(CT):
-            row_f[:, n * CHUNK + t * 128:n * CHUNK + (t + 1) * 128] = total[t:t + 1]
+        put(n, total)
+    take(f2_in.at[1:NX], f2r_sem.at[0])
+    total = f2_own
+    for dx in (1, 3, 2):
+        total = total + f2_in[dx].astype(F32)
+    put(NX1, total)
     out_ref[...] = row_f[...].astype(BF16)
 
     take(q_in.at[0:7], qs_sem.at[0])
@@ -339,6 +370,8 @@
     take(e1_out, e1s_sem.at[0])
     take(e2_out.at[:, 1:NX], e2s_sem.at[0])
     take(e3_out.at[:, 1:NZ], e3s_sem.at[0])
+    take(f1_out.at[1:NZ], f1s_sem.at[0])
+    take(f2_out.at[1:NX], f2s_sem.at[0])
 
 
 def body(queries, lengths, pages, slot_owner, slot_page, value_up, out_proj):
@@ -375,15 +408,21 @@
             pltpu.VMEM((NCH, 32, CHUNK), F32),
             pltpu.VMEM((NCH, 32, CHUNK), BF16),
             pltpu.VMEM((NCH, 32, CHUNK), BF16),
-            pltpu.VMEM((NCH, NX, 16, CHUNK // 2), BF16),
-            pltpu.VMEM((NCH, NX, 16, CHUNK // 2), BF16),
-            pltpu.VMEM((NCH, CT * 8, 128), F32),
-            pltpu.VMEM((NCH, NZ, 16, 128), BF16),
-            pltpu.VMEM((NCH, NZ, 16, 128), BF16),
+            pltpu.VMEM((NX1, NX, 16, CHUNK // 2), BF16),
+            pltpu.VMEM((NX1, NX, 16, CHUNK // 2), BF16),
+            pltpu.VMEM((NX1, CT * 8, 128), F32),
+            pltpu.VMEM((NX1, NZ, 16, 128), BF16),
+            pltpu.VMEM((NX1, NZ, 16, 128), BF16),
+            pltpu.VMEM((512, 128), F32),
+            pltpu.VMEM((NZ, 64, 128), BF16),
+            pltpu.VMEM((NZ, 64, 128), BF16),
+            pltpu.VMEM((64, 128), F32),
+            pltpu.VMEM((NX, 16, 128), BF16),
+            pltpu.VMEM((NX, 16, 128), BF16),
             dma((7,)), pltpu.SemaphoreType.REGULAR((5,)),
             dma((1,)), dma((3,)), dma((2,)), dma((2,)), dma((1,)), dma((3,)), dma((1,)), dma((3,)),
             dma((2,)), dma((GRP,)), dma((2,)), dma((GRP,)), dma((1,)), dma((1,)),
-            dma((1,)), dma((NCH,)), dma((1,)), dma((NCH,)), dma((1,)), dma((NCH,)),
+            dma((1,)), dma((NCH,)), dma((1,)), dma((NX1,)), dma((1,)), dma((NX1,)), dma((1,)), dma((1,)), dma((1,)), dma((1,)),
         ],
         compiler_params=pltpu.CompilerParams(
             collective_id=0, has_side_effects=True, vmem_limit_bytes=60 * 1024 * 1024),

time: 56.2 us -> 54.8 us (0.975)
  Pallas kernels: 54 us -> 52.1 us
    pallas_call x1, Pallas kernels: 54 us -> 52.1 us  [body(): pl.pallas_call(kernel, out_shape=jax.ShapeDtypeStruct((1, D), BF16), in_s...]
where the time goes in v7:
time: 54.8 us; the launch traced here: 54.2 us
  Pallas kernels  52.1 us (95%)
  local copies, waits for them, and re-layouts  1.39 us (3%)
  between operations  0.66 us (1%)
    pallas_call x1, Pallas kernels, body(): pl.pallas_call(kernel, out_shape=jax.ShapeDtypeStruct((1, D), BF16), in_s...  52.1 us
    unnamed x1, local copies, waits for them, and re-layouts  1.39 us

profile of v7, /device:TPU:1, one launch (start us, length us, event | category | flops | bytes accessed | tf_op | source)
XLA Modules:
  0.0 54.2 jit_solution(5436392908922643092)
XLA Ops:
  0.7 52.1 %shard_map.73 = bf16[1,7168]{1,0:T(2,128)(2,1)} custom-call(bf16[1,64,576]{2,1,0:T(8,128)(2,1)} %q_hbm.1, s32[1]{0:T(128)S(6)} %copy.9.len_hbm, bf16[4,64,576]{2,1,0:T(8,128)(2,1)} %pages_hbm.1, s32[4]{0:T(128)} %owner_hbm.1, s32[4]{0:T(128)} %page_hbm.1, bf16[1,512,128]{2,1,0:T(8,128)(2,1)} %vup_hbm.1, bf16[128,7168]{1,0:T(8,128)(2,1)} %oproj_hbm.1), custom_call_target="tpu_custom_call" | custom-call | tf_op jit(solution)/shard_map/pallas_call | solution.py:380
  52.8 1.4 %copy.10 = bf16[1,7168]{1,0:T(2,128)(2,1)} copy(bf16[1,7168]{1,0:T(2,128)(2,1)} %shard_map.73) | data formatting | bytes 28672

commit v8 on v7

--- a/solution.py
+++ b/solution.py
@@ -29,24 +29,15 @@
 D = 7168
 HALF = D // 2
 TILES = D // 128
-NCH = 4
-NX1 = 3
-CHUNK = D // NCH
-CT = CHUNK // 128
-
-
-def pieces(value):
-    high = value.astype(BF16).astype(F32)
-    rest = value - high
-    mid = rest.astype(BF16).astype(F32)
-    return high, mid, rest - mid
+CHUNKS = ((0, 9), (9, 9))
+LAST, LT = 18, 10
 
 
 def kernel(q_hbm, len_hbm, pages_hbm, owner_hbm, page_hbm, vup_hbm, oproj_hbm, out_ref,
            len_ref, owner_ref, page_ref, q_own, q_in, rope_own, rope_in, prope_out, prope_in, meta_own, meta_in, pages, vup, oproj, part_out, part_in, stat_out, stat_in,
-           row_f, lat, c2_out, c2_in, own_f, e1_out, e1_in, e2_out, e2_in, e3_f, e3_out, e3_in, f1_f, f1_out, f1_in, f2_f, f2_out, f2_in,
+           row_f, lat, c2_out, c2_in, own_f, e2_out, e2_in, e3_f, e3_out, e3_in, f1_f, f1_out, f1_in, f2_f, f2_out, f2_in, sent,
            loc_sem, in_sem, ms_sem, mr_sem, gs_sem, gr_sem, qs_sem, qr_sem, rs_sem, rr_sem, ps_sem, pr_sem, ts_sem, tr_sem,
-           c2s_sem, c2r_sem, e1s_sem, e1r_sem, e2s_sem, e2r_sem, e3s_sem, e3r_sem, f1s_sem, f1r_sem, f2s_sem, f2r_sem):
+           c2s_sem, c2r_sem, vs_sem, vr_sem, ws_sem, wr_sem, e2s_sem, e2r_sem, e3s_sem, e3r_sem, f1s_sem, f1r_sem, f2s_sem, f2r_sem):
     g = lax.axis_index("grp")
     d = lax.axis_index("dev")
     z = d // NS
@@ -76,9 +67,12 @@
         load.start()
     pages_load = pltpu.make_async_copy(pages_hbm, pages.at[0:POOL], loc_sem.at[1])
     pages_load.start()
-    vup_load = pltpu.make_async_copy(vup_hbm.at[0], vup, loc_sem.at[2])
+    vup_load = pltpu.make_async_copy(vup_hbm.at[0], vup.at[c], loc_sem.at[2])
     vup_load.start()
-    oproj_load = pltpu.make_async_copy(oproj_hbm, oproj, loc_sem.at[3])
+    def columns(core):
+        return oproj_hbm.at[:, pl.ds(pl.multiple_of(core * HALF, 128), HALF)]
+
+    oproj_load = pltpu.make_async_copy(columns(c), oproj.at[c], loc_sem.at[3])
     oproj_load.start()
 
     def tell(sem, peers):
@@ -145,6 +139,10 @@
     remote(prope_out.at[0], prope_in.at[0], gs_sem.at[1], gr_sem.at[1], grp_peer(1))
     remote(prope_out.at[1], prope_in.at[1], gs_sem.at[1], gr_sem.at[1], grp_peer(7))
     send_sides(1)
+
+    core_peer = (g, z * NS + x * 2 + (1 - c))
+    remote(vup_hbm.at[0], vup.at[c], vs_sem.at[0], vr_sem.at[0], core_peer)
+    remote(columns(1 - c), oproj.at[c], ws_sem.at[0], wr_sem.at[0], core_peer)
     pl.semaphore_wait(in_sem.at[0], 2)
     send_queries(2)
     send_sides(2)
@@ -256,96 +254,101 @@
         for k, factor in zip(sources, factors):
             both = part_in[k, :, :, j % 2 * 128:j % 2 * 128 + 128].astype(F32)
             block = block + factor * both[:, j // 2 * 8:j // 2 * 8 + 8].reshape(HEADS, 128)
-        lat[j] = block
-
-    for ss in range(NS):
-        quarters = [lat[j, pl.ds(ss, NZ, stride=NS), :] for j in range(4)]
-        c2_out[ss] = jnp.concatenate([jnp.concatenate(quarters[0:2], axis=1), jnp.concatenate(quarters[2:4], axis=1)], axis=0).astype(BF16)
+        lat[j, 0:HEADS, :] = block
+
+    for xx in range(NX):
+        for core in range(2):
+            quarters = [lat[j, pl.ds(xx * 2 + core, NZ, stride=NS), :] for j in range(4)]
+            c2_out[xx, core * 16:(core + 1) * 16, :] = jnp.concatenate(
+                [jnp.concatenate(quarters[0:2], axis=1), jnp.concatenate(quarters[2:4], axis=1)], axis=0).astype(BF16)
     for k in order:
-        remote(c2_out.at[lax.rem(s + k, NS)], c2_in.at[s], c2s_sem.at[0], c2r_sem.at[0], s_peer(k))
-    pltpu.make_async_copy(c2_out.at[s], c2_in.at[s], c2r_sem.at[0]).start()
+        to = lax.rem(s + k, NS)
+        remote(c2_out.at[to // 2], c2_in.at[s], c2s_sem.at[0], c2r_sem.at[0], (g, z * NS + to))
+    pltpu.make_async_copy(c2_out.at[x], c2_in.at[s], c2r_sem.at[0]).start()
     vup_load.wait()
+    take(vup.at[0], vr_sem.at[0])
     take(c2_in, c2r_sem.at[0])
 
-    blocks = []
-    for dc in (1, 0):
-        for dx in range(NX):
-            at = lax.rem(x + dx, NX) * 2 + lax.rem(c + dc, 2)
-            both = c2_in[at].astype(F32)
-            blocks.append(jnp.concatenate([both[0:8, :], both[8:16, :]], axis=1))
-    heads_in = jnp.concatenate(blocks, axis=0).astype(BF16)
-    head_value = jnp.dot(heads_in, vup[...], preferred_element_type=F32).astype(BF16)
+    blocks = [[], []]
+    for dx in range(NX):
+        for core in range(2):
+            both = c2_in[lax.rem(x + dx, NX) * 2 + core].astype(F32)
+            for head in range(2):
+                blocks[head].append(jnp.concatenate([both[head * 16:head * 16 + 8], both[head * 16 + 8:head * 16 + 16]], axis=1))
+    head_value = jnp.concatenate(
+        [jnp.dot(jnp.concatenate(blocks[head], axis=0).astype(BF16), vup[head], preferred_element_type=F32) for head in range(2)],
+        axis=1).astype(BF16)
 
     oproj_load.wait()
-    core_peer = (g, z * NS + x * 2 + (1 - c))
-    for n in (NX1, 0, 1, 2):
-        cols = slice(n * CHUNK, (n + 1) * CHUNK)
-        product = jnp.dot(head_value, oproj[:, cols], preferred_element_type=F32)
-        e1_out[n] = product[0:32].astype(BF16)
-        remote(e1_out.at[n], e1_in.at[n], e1s_sem.at[0], e1r_sem.at[n], core_peer)
-        own_f[n] = product[32:64]
-
-    take(e1_in.at[NX1], e1r_sem.at[NX1])
-    both = own_f[NX1] + e1_in[NX1].astype(F32)
-    for t in range(CT):
-        f1_f[t * 32:(t + 1) * 32, :] = both[:, t * 128:(t + 1) * 128]
-    f1_f[CT * 32:512, :] = jnp.zeros((512 - CT * 32, 128), F32)
-    for zz in range(NZ):
-        f1_out[zz] = f1_f[pl.ds(zz, 64, stride=8), :].astype(BF16)
-    for k in order:
-        remote(f1_out.at[lax.rem(z + k, NZ)], f1_in.at[k], f1s_sem.at[0], f1r_sem.at[0], z_peer(k))
-
-    for n in range(NX1):
-        take(e1_in.at[n], e1r_sem.at[n])
-        both = own_f[n] + e1_in[n].astype(F32)
-        own_f[n] = both
+    take(oproj.at[0], wr_sem.at[0])
+
+    def product(first, count):
+        cols = slice(first * 128, (first + count) * 128)
+        return jnp.dot(head_value, oproj[:, :, cols].reshape(2 * VDIM, count * 128), preferred_element_type=F32)
+
+    for n, (first, count) in enumerate(CHUNKS):
+        both = product(first, count)
+        own_f[:, first * 128:(first + count) * 128] = both[0:16]
         for dx in (2, 1, 3):
-            rows = both[dx * 8:(dx + 1) * 8]
-            e2_out[n, dx] = jnp.concatenate([rows[:, 0:CHUNK // 2], rows[:, CHUNK // 2:CHUNK]], axis=0).astype(BF16)
+            cols = slice(first * 128, (first + count) * 128)
+            e2_out[dx, :, cols] = both[dx * 16:(dx + 1) * 16].astype(BF16)
             peer = (g, z * NS + lax.rem(x + dx, NX) * 2 + c)
-            remote(e2_out.at[n, dx], e2_in.at[n, dx], e2s_sem.at[0], e2r_sem.at[n], peer)
-
-    for n in range(NX1):
-        take(e2_in.at[n, 1:NX], e2r_sem.at[n])
-        for t in range(CT):
-            half, col = t // (CT // 2), t % (CT // 2) * 128
-            total = own_f[n, 0:8, t * 128:(t + 1) * 128]
-            for dx in (1, 3, 2):
-                total = total + e2_in[n, dx, :, col:col + 128].astype(F32)[half * 8:half * 8 + 8]
-            e3_f[n, t * 8:(t + 1) * 8, :] = total
+            remote(e2_out.at[dx, :, cols], e2_in.at[dx, :, cols], e2s_sem.at[n], e2r_sem.at[n], peer)
+        if n == 0:
+            both = product(LAST, LT)
+            for t in range(LT):
+                f1_f[t * HEADS:(t + 1) * HEADS, :] = both[:, t * 128:(t + 1) * 128]
+            for zz in range(NZ):
+                f1_out[zz] = f1_f[pl.ds(zz, LT * 8, stride=8), :].astype(BF16)
+            for k in order:
+                remote(f1_out.at[lax.rem(z + k, NZ)], f1_in.at[k], f1s_sem.at[0], f1r_sem.at[0], z_peer(k))
+
+    for n, (first, count) in enumerate(CHUNKS):
+        cols = slice(first * 128, (first + count) * 128)
+        take(e2_in.at[1:NX, :, cols], e2r_sem.at[n])
+        total = own_f[:, cols]
+        for dx in (1, 3, 2):
+            total = total + e2_in[dx, :, cols].astype(F32)
+        for t in range(count):
+            e3_f[n, t * 16:(t + 1) * 16, :] = total[:, t * 128:(t + 1) * 128]
         for zz in range(NZ):
-            e3_out[n, zz] = jnp.concatenate(
-                [e3_f[n, pl.ds(zz, CT, stride=8), :], jnp.zeros((16 - CT, 128), F32)], axis=0).astype(BF16)
+            for core in range(2):
+                rows = e3_f[n, pl.ds(core * 8 + zz, count, stride=16), :]
+                e3_out[n, zz, core] = jnp.concatenate([rows, jnp.zeros((16 - count, 128), F32)], axis=0).astype(BF16)
         for k in order:
             to = lax.rem(z + k, NZ)
-            remote(e3_out.at[n, to], e3_in.at[n, k], e3s_sem.at[0], e3r_sem.at[n], z_peer(k))
+            for core in range(2):
+                remote(e3_out.at[n, to, core], e3_in.at[n, c, k], e3s_sem.at[n], e3r_sem.at[n], (g, to * NS + x * 2 + core))
+        remote(e3_out.at[n, z, 1 - c], e3_in.at[n, c, 0], e3s_sem.at[n], e3r_sem.at[n], core_peer)
+        pltpu.make_async_copy(e3_out.at[n, z, c], e3_in.at[n, c, 0], e3r_sem.at[n]).start()
 
     take(f1_in.at[1:NZ], f1r_sem.at[0])
     total = f1_out[z].astype(F32)
     for k in order:
         total = total + f1_in[k].astype(F32)
-    f2_f[...] = total
+    f2_f[0:80, :] = total
+    for dx in (2, 1, 3, 0):
+        for core in range(2):
+            f2_out[dx, core] = jnp.concatenate([f2_f[pl.ds(dx * 2 + core, 10, stride=8), :], jnp.zeros((6, 128), F32)], axis=0).astype(BF16)
     for dx in (2, 1, 3):
-        f2_out[dx] = f2_f[pl.ds(dx, 16, stride=4), :].astype(BF16)
-        peer = (g, z * NS + lax.rem(x + dx, NX) * 2 + c)
-        remote(f2_out.at[dx], f2_in.at[dx], f2s_sem.at[0], f2r_sem.at[0], peer)
-    f2_own = f2_f[pl.ds(0, 16, stride=4), :]
-
-    def put(n, total):
-        for t in range(CT):
-            row_f[:, n * CHUNK + t * 128:n * CHUNK + (t + 1) * 128] = total[t:t + 1]
-
-    for n in range(NX1):
-        take(e3_in.at[n, 1:NZ], e3r_sem.at[n])
-        total = e3_out[n, z].astype(F32)
-        for k in order:
-            total = total + e3_in[n, k].astype(F32)
-        put(n, total)
-    take(f2_in.at[1:NX], f2r_sem.at[0])
-    total = f2_own
-    for dx in (1, 3, 2):
-        total = total + f2_in[dx].astype(F32)
-    put(NX1, total)
+        for core in range(2):
+            peer = (g, z * NS + lax.rem(x + dx, NX) * 2 + core)
+            remote(f2_out.at[dx, core], f2_in.at[c, dx], f2s_sem.at[0], f2r_sem.at[0], peer)
+    remote(f2_out.at[0, 1 - c], f2_in.at[c, 0], f2s_sem.at[0], f2r_sem.at[0], core_peer)
+    pltpu.make_async_copy(f2_out.at[0, c], f2_in.at[c, 0], f2r_sem.at[0]).start()
+
+    def put(core, first, count, total):
+        for t in range(count):
+            at = core * HALF + (first + t) * 128
+            row_f[:, at:at + 128] = total[t:t + 1]
+
+    for n, (first, count) in enumerate(CHUNKS):
+        take(e3_in.at[n], e3r_sem.at[n])
+        for core in range(2):
+            put(core, first, count, jnp.sum(e3_in[n, core].astype(F32), axis=0))
+    take(f2_in, f2r_sem.at[0])
+    for core in range(2):
+        put(core, LAST, LT, jnp.sum(f2_in[core].astype(F32), axis=0))
     out_ref[...] = row_f[...].astype(BF16)
 
     take(q_in.at[0:7], qs_sem.at[0])
@@ -366,12 +369,14 @@
         take(part_out.at[0], ps_sem.at[0])
         take(stat_in.at[0, 0:4], ts_sem.at[0])
 
-    take(c2_out.at[1:NS], c2s_sem.at[0])
-    take(e1_out, e1s_sem.at[0])
-    take(e2_out.at[:, 1:NX], e2s_sem.at[0])
-    take(e3_out.at[:, 1:NZ], e3s_sem.at[0])
+    take(c2_in.at[1:NS], c2s_sem.at[0])
+    take(vup.at[0], vs_sem.at[0])
+    take(oproj.at[0], ws_sem.at[0])
+    for n, (first, count) in enumerate(CHUNKS):
+        take(e2_out.at[1:NX, :, first * 128:(first + count) * 128], e2s_sem.at[n])
+        take(sent.at[0:15], e3s_sem.at[n])
     take(f1_out.at[1:NZ], f1s_sem.at[0])
-    take(f2_out.at[1:NX], f2s_sem.at[0])
+    take(sent.at[0:7], f2s_sem.at[0])
 
 
 def body(queries, lengths, pages, slot_owner, slot_page, value_up, out_proj):
@@ -395,34 +400,34 @@
             pltpu.VMEM((1, 128), jnp.int32),
             pltpu.VMEM((GRP, 1, 128), jnp.int32),
             pltpu.VMEM((2 * POOL, PAGE, CACHE), BF16),
-            pltpu.VMEM((LAT, VDIM), BF16),
-            pltpu.VMEM((VDIM, D), BF16),
+            pltpu.VMEM((2, LAT, VDIM), BF16),
+            pltpu.VMEM((2, VDIM, HALF), BF16),
             pltpu.VMEM((GRP, 4, 16, 256), BF16),
             pltpu.VMEM((GRP, NZ, 16, 256), BF16),
             pltpu.VMEM((GRP, 2, 128), F32),
             pltpu.VMEM((GRP, NZ, 2, 128), F32),
             pltpu.VMEM((1, D), F32),
-            pltpu.VMEM((4, HEADS, 128), F32),
-            pltpu.VMEM((NS, 16, 256), BF16),
-            pltpu.VMEM((NS, 16, 256), BF16),
-            pltpu.VMEM((NCH, 32, CHUNK), F32),
-            pltpu.VMEM((NCH, 32, CHUNK), BF16),
-            pltpu.VMEM((NCH, 32, CHUNK), BF16),
-            pltpu.VMEM((NX1, NX, 16, CHUNK // 2), BF16),
-            pltpu.VMEM((NX1, NX, 16, CHUNK // 2), BF16),
-            pltpu.VMEM((NX1, CT * 8, 128), F32),
-            pltpu.VMEM((NX1, NZ, 16, 128), BF16),
-            pltpu.VMEM((NX1, NZ, 16, 128), BF16),
-            pltpu.VMEM((512, 128), F32),
-            pltpu.VMEM((NZ, 64, 128), BF16),
-            pltpu.VMEM((NZ, 64, 128), BF16),
-            pltpu.VMEM((64, 128), F32),
-            pltpu.VMEM((NX, 16, 128), BF16),
-            pltpu.VMEM((NX, 16, 128), BF16),
+            pltpu.VMEM((4, HEADS + 8, 128), F32),
+            pltpu.VMEM((NX, 32, 256), BF16),
+            pltpu.VMEM((NS, 32, 256), BF16),
+            pltpu.VMEM((16, LAST * 128), F32),
+            pltpu.VMEM((NX, 16, LAST * 128), BF16),
+            pltpu.VMEM((NX, 16, LAST * 128), BF16),
+            pltpu.VMEM((2, 14 * 16 + 16, 128), F32),
+            pltpu.VMEM((2, NZ, 2, 16, 128), BF16),
+            pltpu.VMEM((2, 2, NZ, 16, 128), BF16),
+            pltpu.VMEM((LT * HEADS + 8, 128), F32),
+            pltpu.VMEM((NZ, 80, 128), BF16),
+            pltpu.VMEM((NZ, 80, 128), BF16),
+            pltpu.VMEM((80+8, 128), F32),
+            pltpu.VMEM((NX, 2, 16, 128), BF16),
+            pltpu.VMEM((2, NX, 16, 128), BF16),
+            pltpu.VMEM((16, 16, 128), BF16),
             dma((7,)), pltpu.SemaphoreType.REGULAR((5,)),
             dma((1,)), dma((3,)), dma((2,)), dma((2,)), dma((1,)), dma((3,)), dma((1,)), dma((3,)),
-            dma((2,)), dma((GRP,)), dma((2,)), dma((GRP,)), dma((1,)), dma((1,)),
-            dma((1,)), dma((NCH,)), dma((1,)), dma((NX1,)), dma((1,)), dma((NX1,)), dma((1,)), dma((1,)), dma((1,)), dma((1,)),
+            dma((2,)), dma((GRP,)), dma((2,)), dma((GRP,)),
+            dma((1,)), dma((1,)), dma((1,)), dma((1,)), dma((1,)), dma((1,)),
+            dma((2,)), dma((2,)), dma((2,)), dma((2,)), dma((1,)), dma((1,)), dma((1,)), dma((1,)),
         ],
         compiler_params=pltpu.CompilerParams(
             collective_id=0, has_side_effects=True, vmem_limit_bytes=60 * 1024 * 1024),

time: 54.8 us -> 54 us (0.985)
  no operation moved by 1% of the time
where the time goes in v8:
time: 54 us; the launch traced here: 53.8 us
  Pallas kernels  51.8 us (96%)
  local copies, waits for them, and re-layouts  1.39 us (3%)
  between operations  0.66 us (1%)
    pallas_call x1, Pallas kernels, body(): pl.pallas_call(kernel, out_shape=jax.ShapeDtypeStruct((1, D), BF16), in_s...  51.8 us
    unnamed x1, local copies, waits for them, and re-layouts  1.39 us

profile of v8, /device:TPU:1, one launch (start us, length us, event | category | flops | bytes accessed | tf_op | source)
XLA Modules:
  0.0 53.8 jit_solution(13234841767239563648)
XLA Ops:
  0.7 51.8 %shard_map.73 = bf16[1,7168]{1,0:T(2,128)(2,1)} custom-call(bf16[1,64,576]{2,1,0:T(8,128)(2,1)} %q_hbm.1, s32[1]{0:T(128)S(6)} %copy.9.len_hbm, bf16[4,64,576]{2,1,0:T(8,128)(2,1)} %pages_hbm.1, s32[4]{0:T(128)} %owner_hbm.1, s32[4]{0:T(128)} %page_hbm.1, bf16[1,512,128]{2,1,0:T(8,128)(2,1)} %vup_hbm.1, bf16[128,7168]{1,0:T(8,128)(2,1)} %oproj_hbm.1), custom_call_target="tpu_custom_call" | custom-call | tf_op jit(solution)/shard_map/pallas_call | solution.py:385
  52.4 1.4 %copy.10 = bf16[1,7168]{1,0:T(2,128)(2,1)} copy(bf16[1,7168]{1,0:T(2,128)(2,1)} %shard_map.73) | data formatting | bytes 28672

commit v9 on v8

--- a/solution.py
+++ b/solution.py
@@ -55,7 +55,8 @@
         return (g, z * NS + lax.rem(s + k, NS))
 
     barrier = pltpu.get_barrier_semaphore()
-    near = [f(k) for f in (grp_peer, z_peer) for k in (1, 7, 2, 6)] + [s_peer(k) for k in range(1, 8)]
+    core_peer = (g, z * NS + x * 2 + (1 - c))
+    near = [grp_peer(1), grp_peer(7), z_peer(1), z_peer(7), s_peer(2), s_peer(6), core_peer]
     for peer in near:
         pl.semaphore_signal(barrier, inc=1, device_id=peer, device_id_type=MESH)
 
@@ -127,26 +128,31 @@
     for side in range(2):
         rope = [pages[2 * side + i, :, LAT:CACHE].astype(F32) for i in range(2)]
         prope_out[side] = jnp.concatenate(rope, axis=1).astype(BF16)
-    pl.semaphore_wait(barrier, 15)
-    tell(in_sem.at[0], [grp_peer(2), grp_peer(6)])
-    tell(in_sem.at[1], [z_peer(2), z_peer(6)])
+
+    pl.semaphore_wait(barrier, 7)
+    tell(in_sem.at[0], [grp_peer(1), grp_peer(7)])
+    tell(in_sem.at[1], [z_peer(1), z_peer(7)])
+    tell(in_sem.at[6], [s_peer(2), s_peer(6), core_peer])
     send_queries(0)
-    send_queries(1)
+    send_sides(0)
     remote(pages.at[0:2, :, 0:LAT], pages.at[4:6, :, 0:LAT], gs_sem.at[0], gr_sem.at[0], grp_peer(1))
     remote(pages.at[2:4, :, 0:LAT], pages.at[6:8, :, 0:LAT], gs_sem.at[0], gr_sem.at[0], grp_peer(7))
-
-    send_sides(0)
     remote(prope_out.at[0], prope_in.at[0], gs_sem.at[1], gr_sem.at[1], grp_peer(1))
     remote(prope_out.at[1], prope_in.at[1], gs_sem.at[1], gr_sem.at[1], grp_peer(7))
-    send_sides(1)
-
-    core_peer = (g, z * NS + x * 2 + (1 - c))
     remote(vup_hbm.at[0], vup.at[c], vs_sem.at[0], vr_sem.at[0], core_peer)
     remote(columns(1 - c), oproj.at[c], ws_sem.at[0], wr_sem.at[0], core_peer)
     pl.semaphore_wait(in_sem.at[0], 2)
+    tell(in_sem.at[5], [grp_peer(2), grp_peer(6)])
+    send_queries(1)
+    send_sides(1)
+    pl.semaphore_wait(in_sem.at[1], 2)
+    tell(in_sem.at[7], [z_peer(2), z_peer(6)])
+    pl.semaphore_wait(in_sem.at[6], 3)
+    tell(in_sem.at[8], [s_peer(2), s_peer(6)])
+    pl.semaphore_wait(in_sem.at[5], 2)
     send_queries(2)
     send_sides(2)
-    pl.semaphore_wait(in_sem.at[1], 2)
+    pl.semaphore_wait(in_sem.at[7], 2)
     for at in range(3):
         tell(in_sem.at[2 + at], [grp_peer(k) for k in groups[at]])
 
@@ -261,6 +267,7 @@
             quarters = [lat[j, pl.ds(xx * 2 + core, NZ, stride=NS), :] for j in range(4)]
             c2_out[xx, core * 16:(core + 1) * 16, :] = jnp.concatenate(
                 [jnp.concatenate(quarters[0:2], axis=1), jnp.concatenate(quarters[2:4], axis=1)], axis=0).astype(BF16)
+    pl.semaphore_wait(in_sem.at[8], 2)
     for k in order:
         to = lax.rem(s + k, NS)
         remote(c2_out.at[to // 2], c2_in.at[s], c2s_sem.at[0], c2r_sem.at[0], (g, z * NS + to))
@@ -423,7 +430,7 @@
             pltpu.VMEM((NX, 2, 16, 128), BF16),
             pltpu.VMEM((2, NX, 16, 128), BF16),
             pltpu.VMEM((16, 16, 128), BF16),
-            dma((7,)), pltpu.SemaphoreType.REGULAR((5,)),
+            dma((7,)), pltpu.SemaphoreType.REGULAR((9,)),
             dma((1,)), dma((3,)), dma((2,)), dma((2,)), dma((1,)), dma((3,)), dma((1,)), dma((3,)),
             dma((2,)), dma((GRP,)), dma((2,)), dma((GRP,)),
             dma((1,)), dma((1,)), dma((1,)), dma((1,)), dma((1,)), dma((1,)),

time: 54 us -> 53.3 us (0.987)
  Pallas kernels: 51.8 us -> 51 us
    pallas_call x1, Pallas kernels: 51.8 us -> 51 us  [body(): pl.pallas_call(kernel, out_shape=jax.ShapeDtypeStruct((1, D), BF16), in_s...]
where the time goes in v9:
time: 53.3 us; the launch traced here: 53.1 us
  Pallas kernels  51 us (96%)
  local copies, waits for them, and re-layouts  1.39 us (3%)
  between operations  0.66 us (1%)
    pallas_call x1, Pallas kernels, body(): pl.pallas_call(kernel, out_shape=jax.ShapeDtypeStruct((1, D), BF16), in_s...  51 us
    unnamed x1, local copies, waits for them, and re-layouts  1.39 us

profile of v9, /device:TPU:1, one launch (start us, length us, event | category | flops | bytes accessed | tf_op | source)
XLA Modules:
  0.0 53.1 jit_solution(10153359530949537289)
XLA Ops:
  0.7 51.0 %shard_map.73 = bf16[1,7168]{1,0:T(2,128)(2,1)} custom-call(bf16[1,64,576]{2,1,0:T(8,128)(2,1)} %q_hbm.1, s32[1]{0:T(128)S(6)} %copy.9.len_hbm, bf16[4,64,576]{2,1,0:T(8,128)(2,1)} %pages_hbm.1, s32[4]{0:T(128)} %owner_hbm.1, s32[4]{0:T(128)} %page_hbm.1, bf16[1,512,128]{2,1,0:T(8,128)(2,1)} %vup_hbm.1, bf16[128,7168]{1,0:T(8,128)(2,1)} %oproj_hbm.1), custom_call_target="tpu_custom_call" | custom-call | tf_op jit(solution)/shard_map/pallas_call | solution.py:392
  51.7 1.4 %copy.10 = bf16[1,7168]{1,0:T(2,128)(2,1)} copy(bf16[1,7168]{1,0:T(2,128)(2,1)} %shard_map.73) | data formatting | bytes 28672

commit v10 on v9

--- a/solution.py
+++ b/solution.py
@@ -239,28 +239,26 @@
     odd = lax.rem(g + z // 4, 2)
     sources = [even_k + odd * (odd_k - even_k) for even_k, odd_k in ((0, 1), (2, 7), (6, 3), (4, 5))]
     mine = lane64 == lax.rem(z, 4) * 8 + lax.broadcasted_iota(jnp.int32, (HEADS, 128), 0) % 8
-    tops, totals = [], []
-    for k in sources:
+    state = None
+    for at, k in enumerate(sources):
         take(stat_in.at[k], tr_sem.at[k])
         take(part_in.at[k], pr_sem.at[k])
-        for at, columns in enumerate((tops, totals)):
-            spread = jnp.broadcast_to(stat_in[k, :, at:at + 1, :], (NZ, 8, 128)).reshape(HEADS, 128)
-            columns.append(jnp.sum(jnp.where(mine, spread, 0.0), axis=1, keepdims=True))
-    best = tops[0]
-    for top in tops[1:]:
-        best = jnp.maximum(best, top)
-    factors = [jnp.exp(top - best) for top in tops]
-    denominator = 0.0
-    for factor, total in zip(factors, totals):
-        denominator = denominator + factor * total
-    scale = 1.0 / denominator
-    factors = [factor * scale for factor in factors]
-    for j in range(4):
-        block = 0.0
-        for k, factor in zip(sources, factors):
+        top, total = [jnp.sum(jnp.where(mine, jnp.broadcast_to(stat_in[k, :, i:i + 1, :], (NZ, 8, 128)).reshape(HEADS, 128), 0.0),
+                              axis=1, keepdims=True) for i in range(2)]
+        if at == 0:
+            old_factor, factor = None, 1.0
+            state = (top, total)
+        else:
+            best = jnp.maximum(state[0], top)
+            old_factor, factor = jnp.exp(state[0] - best), jnp.exp(top - best)
+            state = (best, old_factor * state[1] + factor * total)
+            if at == 3:
+                scale = 1.0 / state[1]
+                old_factor, factor = old_factor * scale, factor * scale
+        for j in range(4):
             both = part_in[k, :, :, j % 2 * 128:j % 2 * 128 + 128].astype(F32)
-            block = block + factor * both[:, j // 2 * 8:j // 2 * 8 + 8].reshape(HEADS, 128)
-        lat[j, 0:HEADS, :] = block
+            block = both[:, j // 2 * 8:j // 2 * 8 + 8].reshape(HEADS, 128)
+            lat[j, 0:HEADS, :] = block if at == 0 else old_factor * lat[j, 0:HEADS, :] + factor * block
 
     for xx in range(NX):
         for core in range(2):

time: 53.3 us -> 53.2 us (level)
  no operation moved by 1% of the time
where the time goes in v10:
time: 53.2 us; the launch traced here: 53 us
  Pallas kernels  51 us (96%)
  local copies, waits for them, and re-layouts  1.39 us (3%)
  between operations  0.66 us (1%)
    pallas_call x1, Pallas kernels, body(): pl.pallas_call(kernel, out_shape=jax.ShapeDtypeStruct((1, D), BF16), in_s...  51 us
    unnamed x1, local copies, waits for them, and re-layouts  1.39 us

profile of v10, /device:TPU:1, one launch (start us, length us, event | category | flops | bytes accessed | tf_op | source)
XLA Modules:
  0.0 53.0 jit_solution(16186425525400845791)
XLA Ops:
  0.7 51.0 %shard_map.73 = bf16[1,7168]{1,0:T(2,128)(2,1)} custom-call(bf16[1,64,576]{2,1,0:T(8,128)(2,1)} %q_hbm.1, s32[1]{0:T(128)S(6)} %copy.9.len_hbm, bf16[4,64,576]{2,1,0:T(8,128)(2,1)} %pages_hbm.1, s32[4]{0:T(128)} %owner_hbm.1, s32[4]{0:T(128)} %page_hbm.1, bf16[1,512,128]{2,1,0:T(8,128)(2,1)} %vup_hbm.1, bf16[128,7168]{1,0:T(8,128)(2,1)} %oproj_hbm.1), custom_call_target="tpu_custom_call" | custom-call | tf_op jit(solution)/shard_map/pallas_call | solution.py:390
  51.7 1.4 %copy.10 = bf16[1,7168]{1,0:T(2,128)(2,1)} copy(bf16[1,7168]{1,0:T(2,128)(2,1)} %shard_map.73) | data formatting | bytes 28672
